TPU v7x, 128 devices: a whole 4x4x4 slice. The times are simulated.
128 devices in a mesh: req: 8 (over z, core), pos: 16 (over y, x).
Axes of the slice: x: 4, y: 4, z: 4, core: 2. Of those that a mesh axis runs over, the one named last changes fastest.
Arguments:
- res_latent: bfloat16 [48, 16, 1024, 576], P('req', 'pos'), may hold values from -8 to 8
- res_index: bfloat16 [48, 16, 1024, 128], P('req', 'pos'), may hold values from -6 to 6
- res_len: int32 [48], P('req'), may hold values from 8193 to 16384
- arrive_latent: bfloat16 [32, 16384, 576], P('req', 'pos'), may hold values from -8 to 8
- arrive_index: bfloat16 [32, 16384, 128], P('req', 'pos'), may hold values from -6 to 6
- arrive_len: int32 [32], replicated, may hold values from 8193 to 16384
- destination: int32 [32], replicated, may hold values from 0 to 7, as said below
- q_nope: bfloat16 [4, 80, 128, 128], P(None, 'req', 'pos'), may hold values from -6 to 6
- q_rope: bfloat16 [4, 80, 128, 64], P(None, 'req', 'pos'), may hold values from -18 to 18
- w_uk: bfloat16 [128, 128, 512], P('pos'), may hold values from -0.5 to 0.5
- w_uv: bfloat16 [128, 512, 128], P('pos'), may hold values from -3 to 3
- idx_query: bfloat16 [4, 80, 64, 128], P(None, 'req', 'pos'), may hold values from -6 to 6
- idx_weight: bfloat16 [4, 80, 64], P(None, 'req', 'pos'), may hold values from -0.75 to 0.75
- selected: int32 [4, 80, 32], P(None, 'req'), may hold values from 0 to 127, as said below
Outputs:
- arrived_latent: bfloat16 [32, 16, 1024, 576], P('req', 'pos')
- arrived_index: bfloat16 [32, 16, 1024, 128], P('req', 'pos')
- index_scores: float32 [4, 80, 16, 1024], P(None, 'req', 'pos')
- head_out: bfloat16 [4, 80, 128, 128], P(None, 'req', 'pos')
Inputs may be any that keep to these rules, and one draw needn't show every extreme that they name: `destination`: for each k < 4, the finished prefills s * 4 + k over all s go to different groups, and the 4 prefills of one group s go to different groups. `selected`: each row names 32 different pages. At most 8 pages of a row are equal modulo 16, and every row has exactly 8 pages equal modulo 16.
All inputs are finite; a program needn't handle non-finite values.
Results may differ from a plain program's by a relative error of at most 0.025.
Values may be sent and summed in bfloat16 or wider, within the bound.
A program may use at most 192 MiB of HBM per device.

v0:
```python
import jax
import jax.numpy as jnp
from jax import lax
from jax.sharding import PartitionSpec as P

KV = 512
ROPE = 64
NOPE = 128
IDIM = 128
PAGE = 64
PG_LOC = 16
SEL_MOST = 8


def outgoing_pages(prefill_rows, within, chosen_rows, occupied, req_count, pos_count):
    lane_width = prefill_rows.shape[-1]
    zero_value = jnp.zeros((), prefill_rows.dtype)
    masked = jnp.where(within[:, :, None], prefill_rows, zero_value)
    routed = jnp.where(occupied[:, None, None], masked[chosen_rows], zero_value)
    per_pair = PG_LOC // pos_count
    paged = routed.reshape(req_count, per_pair, pos_count, PAGE, lane_width).transpose(
        0, 2, 1, 3, 4
    )
    return paged.reshape(req_count, pos_count, per_pair * PAGE, lane_width)


def index_part(queries, weights, index_keys):
    logits = jnp.einsum("sbhd,bld->sbhl", queries, index_keys, preferred_element_type=jnp.float32)
    scored = jnp.einsum(
        "sbhl,sbh->sbl",
        jnp.maximum(logits, 0.0),
        weights.astype(jnp.float32),
        precision=lax.Precision.HIGHEST,
    )
    return scored * IDIM ** (-0.5)


def body(
    res_latent,
    res_index,
    res_len,
    arrive_latent,
    arrive_index,
    arrive_len,
    destination,
    q_nope,
    q_rope,
    w_uk,
    w_uv,
    idx_query,
    idx_weight,
    selected,
):
    req_count = lax.axis_size("req")
    pos_count = lax.axis_size("pos")
    req_index = lax.axis_index("req")
    pos_index = lax.axis_index("pos")
    arrivals = arrive_latent.shape[0]
    resident = res_latent.shape[0]
    ctx_local = arrive_latent.shape[1]
    lat_width = arrive_latent.shape[2]
    idx_width = arrive_index.shape[2]
    routing = destination.reshape(req_count, arrivals)
    group_ids = jnp.arange(req_count, dtype=jnp.int32)
    arrival_ids = jnp.arange(arrivals, dtype=jnp.int32)
    outbound = routing[req_index]
    source_lengths = lax.dynamic_slice_in_dim(arrive_len, req_index * arrivals, arrivals)
    positions = pos_index * ctx_local + jnp.arange(ctx_local, dtype=jnp.int32)
    within = positions[None, :] < source_lengths[:, None]
    matches = outbound[None, :] == group_ids[:, None]
    chosen_rows = jnp.sum(jnp.where(matches, arrival_ids[None, :], 0), axis=1)
    occupied = jnp.any(matches, axis=1)
    send_latent = outgoing_pages(arrive_latent, within, chosen_rows, occupied, req_count, pos_count)
    send_index = outgoing_pages(arrive_index, within, chosen_rows, occupied, req_count, pos_count)
    flat_latent, flat_index = (
        lax.all_to_all(
            send_latent.reshape(req_count * pos_count, -1, lat_width),
            ("req", "pos"),
            split_axis=0,
            concat_axis=0,
            tiled=True,
        ),
        lax.all_to_all(
            send_index.reshape(req_count * pos_count, -1, idx_width),
            ("req", "pos"),
            split_axis=0,
            concat_axis=0,
            tiled=True,
        ),
    )
    got_latent = flat_latent.reshape(req_count, pos_count, -1, lat_width)
    got_index = flat_index.reshape(req_count, pos_count, -1, idx_width)
    inbound = routing == req_index
    sources = jnp.sum(jnp.where(inbound, group_ids[:, None], 0), axis=0)
    new_latent = got_latent[sources].reshape(arrivals, ctx_local, lat_width)
    new_index = got_index[sources].reshape(arrivals, ctx_local, idx_width)
    new_lengths = arrive_len[sources * arrivals + arrival_ids]
    gathered_query, gathered_weight = (
        lax.all_gather(idx_query, "pos", axis=2, tiled=True),
        lax.all_gather(idx_weight, "pos", axis=2, tiled=True),
    )
    scored = jnp.concatenate(
        [
            index_part(
                gathered_query[:, :resident], gathered_weight[:, :resident], res_index[:, 0]
            ),
            index_part(gathered_query[:, resident:], gathered_weight[:, resident:], new_index),
        ],
        axis=1,
    )
    lengths = jnp.concatenate([res_len, new_lengths])
    offsets = jnp.arange(ctx_local, dtype=jnp.int32)
    logical = (offsets // PAGE * pos_count + pos_index) * PAGE + offsets % PAGE
    index_scores = jnp.where(logical[None, None, :] < lengths[None, :, None], scored, 0.0)[
        :, :, None, :
    ]
    absorbed = jnp.einsum(
        "sbhn,hnc->sbhc", q_nope, w_uk, preferred_element_type=jnp.float32
    ).astype(jnp.bfloat16)
    queries = jnp.concatenate([absorbed, q_rope], axis=-1)
    owners = selected % pos_count
    local_pages = selected // pos_count
    mine = owners == pos_index
    ranks = jnp.cumsum(mine.astype(jnp.int32), axis=-1) - 1
    slot_ids = jnp.arange(SEL_MOST, dtype=jnp.int32)
    placed = mine[..., None] & (ranks[..., None] == slot_ids)
    slot_pages = jnp.sum(jnp.where(placed, local_pages[..., None], 0), axis=2)
    filled = jnp.any(placed, axis=2)
    res_pages = res_latent[:, 0].reshape(resident, PG_LOC, PAGE, lat_width)
    new_pages = new_latent.reshape(arrivals, PG_LOC, PAGE, lat_width)
    rows_res = res_pages[
        jnp.arange(resident, dtype=jnp.int32)[None, :, None], slot_pages[:, :resident]
    ]
    rows_new = new_pages[arrival_ids[None, :, None], slot_pages[:, resident:]]
    steps_count = selected.shape[0]
    batch_count = resident + arrivals
    attended = jnp.concatenate([rows_res, rows_new], axis=1).reshape(
        steps_count, batch_count, SEL_MOST * PAGE, lat_width
    )
    values = attended[..., :KV]
    live = jnp.repeat(filled, PAGE, axis=-1)
    score_scale = (NOPE + ROPE) ** (-0.5)
    scores = (
        jnp.einsum(
            "sbhc,sbtc->sbht",
            lax.all_gather(queries, "pos", axis=2, tiled=True),
            attended,
            preferred_element_type=jnp.float32,
        )
        * score_scale
    )
    scores = jnp.where(live[:, :, None, :], scores, -1e30)
    largest = jnp.max(scores, axis=-1)
    exponent = jnp.where(live[:, :, None, :], jnp.exp(scores - largest[..., None]), 0.0)
    totals = jnp.sum(exponent, axis=-1)
    numer = jnp.einsum(
        "sbht,sbtc->sbhc", exponent.astype(jnp.bfloat16), values, preferred_element_type=jnp.float32
    )
    largest, totals, numer = (largest, totals, numer)
    overall = lax.pmax(largest, "pos")
    factor = jnp.exp(largest - overall)
    numer_own, total_own = (
        lax.psum_scatter(
            (numer * factor[..., None]).astype(jnp.bfloat16), "pos", scatter_dimension=2, tiled=True
        ).astype(jnp.float32),
        lax.psum_scatter(
            (totals * factor).astype(jnp.bfloat16), "pos", scatter_dimension=2, tiled=True
        ).astype(jnp.float32),
    )
    latent = (numer_own / total_own[..., None]).astype(jnp.bfloat16)
    head_out = jnp.einsum(
        "sbhc,hcd->sbhd", latent, w_uv, preferred_element_type=jnp.float32
    ).astype(jnp.bfloat16)
    return (new_latent[:, None], new_index[:, None], index_scores, head_out)


def solution(mesh):
    placed = (
        P("req", "pos", None, None),
        P("req", "pos", None, None),
        P("req"),
        P("req", "pos", None),
        P("req", "pos", None),
        P(),
        P(),
        P(None, "req", "pos", None),
        P(None, "req", "pos", None),
        P("pos", None, None),
        P("pos", None, None),
        P(None, "req", "pos", None),
        P(None, "req", "pos"),
        P(None, "req", None),
    )
    return jax.shard_map(
        body,
        mesh=mesh,
        in_specs=placed,
        out_specs=(
            P("req", "pos", None, None),
            P("req", "pos", None, None),
            P(None, "req", "pos", None),
            P(None, "req", "pos", None),
        ),
        check_vma=False,
    )
```

profile of v0, /device:TPU:0, one launch (start us, length us, event | category | flops | bytes accessed | tf_op | source)
XLA Modules:
  0.0 560.7 jit_solution(8487124579041223308)
XLA Ops:
  7.2 0.8 reshape.212
  8.0 0.1 select_reduce_fusion.2
  8.3 0.7 dynamic_slice.7
  9.1 4.8 broadcast_select_fusion.1
  14.0 7.4 %gather_fusion = bf16[8,1024,576]{1,2,0:T(8,128)(2,1)} fusion(bf16[4,1024,576]{1,2,0:T(8,128)(2,1)} %broadcast_select_fusion.1, s32[1024]{0:T(1024)S(1)} %pad_clamp_fusion.2), kind=kCustom, calls=%fused_computation | custom fusion | bytes 18874400 | tf_op jit(solution)/shard_map/gather | solution.py:19
  21.3 14.1 %copy.105 = bf16[8,1024,576]{2,1,0:T(8,128)(2,1)} copy(bf16[8,1024,576]{1,2,0:T(8,128)(2,1)} %gather_fusion) | data formatting | bytes 18874368 | tf_op jit(solution)/shard_map/gather | solution.py:19
  35.6 10.0 %broadcast_select_fusion = bf16[128,64,576]{2,1,0:T(8,128)(2,1)} fusion(bf16[128,64,576]{2,1,0:T(8,128)(2,1)} %bitcast.100, pred[128]{0:T(512)(128)(4,1)S(1)} %broadcast_in_dim.162), kind=kLoop, calls=%fused_computation.13 | loop fusion | flops 4718592 | bytes 18874496 | tf_op jit(solution)/shard_map/jit(_where)/select_n | solution.py:19
  45.6 11.6 %all-to-all-start = ((bf16[128,64,576]{2,1,0:T(8,128)(2,1)}), bf16[128,64,576]{2,1,0:T(8,128)(2,1)}, u32[]{:S(2)}, u32[]{:S(2)}) async-start(bf16[128,64,576]{2,1,0:T(8,128)(2,1)} %broadcast_select_fusion), calls=%async_computation | async-start | bytes 20971520 | tf_op jit(solution)/shard_map/all_to_all | solution.py:76
  57.3 1.5 fusion.22
  59.0 0.9 copy.117
  59.9 0.2 all-reduce.4.cloned.1.call-start
  60.2 0.8 reduce_window_sum.11
  61.0 0.8 select_reduce_fusion
  61.9 10.2 %copy.118 = bf16[6,1,1024,576]{3,2,0,1:T(8,128)(2,1)} copy(bf16[6,1,1024,576]{2,3,1,0:T(8,128)(2,1)} %param.14) | data formatting | bytes 14155776 | tf_op args[0]
  72.1 0.8 fusion.30
  73.0 0.1 broadcast_in_dim.176
  73.1 13.7 %gather_fusion.5 = bf16[192,64,576]{2,1,0:T(8,128)(2,1)} fusion(bf16[6,16,64,576]{3,2,1,0:T(8,128)(2,1)} %bitcast.98, s32[192]{0:T(256)S(1)} %reshape.257), kind=kCustom, calls=%fused_computation.5 | custom fusion | bytes 28313088 | tf_op jit(solution)/shard_map/gather | solution.py:131
  86.8 117.7 %all-to-all-done = bf16[128,64,576]{2,1,0:T(8,128)(2,1)} async-done(((bf16[128,64,576]{2,1,0:T(8,128)(2,1)}), bf16[128,64,576]{2,1,0:T(8,128)(2,1)}, u32[]{:S(2)}, u32[]{:S(2)}) %all-to-all-start) | async-done | bytes 9437216 | tf_op jit(solution)/shard_map/all_to_all | solution.py:76
  204.5 7.6 %gather_fusion.1 = bf16[4,16,64,576]{3,2,1,0:T(8,128)(2,1)} fusion(bf16[8,16,64,576]{3,2,1,0:T(8,128)(2,1)} %bitcast.4, s32[1024]{0:T(1024)S(1)} %pad_clamp_fusion.1), kind=kCustom, calls=%fused_computation.1 | custom fusion | bytes 9437200 | tf_op jit(solution)/shard_map/gather | solution.py:95
  212.1 10.3 %gather_fusion.6 = bf16[128,64,576]{2,1,0:T(8,128)(2,1)} fusion(bf16[4,16,64,576]{3,2,1,0:T(8,128)(2,1)} %gather_fusion.1, s32[128]{0:T(128)S(1)} %reshape.263), kind=kCustom, calls=%fused_computation.6 | custom fusion | bytes 18875392 | tf_op jit(solution)/shard_map/gather | solution.py:134
  222.4 17.9 %pad_maximum_fusion = bf16[4,10,8,64,576]{4,3,2,1,0:T(8,128)(2,1)} fusion(bf16[4,4,8,64,576]{4,3,2,1,0:T(8,128)(2,1)} %bitcast.101, bf16[4,6,8,64,576]{4,3,2,1,0:T(8,128)(2,1)} %bitcast.99), kind=kLoop, calls=%fused_computation.7 | loop fusion | flops 11796480 | bytes 47185920 | tf_op jit(solution)/shard_map/concatenate | solution.py:137
  240.4 20.2 %fusion.2 = (f32[4,10,128]{2,1,0:T(8,128)S(1)}, f32[4,10,128,512]{3,2,1,0:T(8,128)}) fusion(pred[4,10,512]{2,1,0:T(8,128)(4,1)S(1)} %copy.114, bf16[4,10,512,576]{3,2,1,0:T(8,128)(2,1)} %bitcast.95, bf16[4,10,128,576]{3,0,1,2:T(4,128)(2,1)} %all-gather.2.cloned.1.call-done), kind=kOutput, calls=%fused_computation.14 | convolution fusion | flops 3027758080 | bytes 40017920 | tf_op jit(solution)/shard_map/sbhc,sbtc->sbht/dot_general | solution.py:144
  260.5 83.2 %pmax.7 = f32[4,10,128]{2,1,0:T(8,128)S(1)} all-reduce(f32[4,10,128]{2,1,0:T(8,128)S(1)} %get-tuple-element.34), channel_id=1, replica_groups=mesh['req'=8,'pos'=16] {'pos'}, use_global_device_ids=true, to_apply=%region_7.8 | all-reduce | flops 5120 | bytes 40960 | tf_op jit(solution)/shard_map/pmax | solution.py:160
  343.8 6.2 %fusion.3 = f32[4,10,128]{2,1,0:T(8,128)S(1)} fusion(f32[4,10,128,512]{3,2,1,0:T(8,128)} %get-tuple-element.35, f32[4,10,128]{2,1,0:T(8,128)S(1)} %get-tuple-element.34, pred[4,10,512]{2,1,0:T(8,128)(4,1)S(1)} %copy.114), kind=kLoop, calls=%fused_computation.15 | loop fusion | flops 13102080 | bytes 10547200 | tf_op jit(solution)/shard_map/reduce_sum | solution.py:155
  350.0 15.0 %multiply_convert_fusion = bf16[4,10,128,512]{3,2,1,0:T(8,128)(2,1)} fusion(f32[4,10,128]{2,1,0:T(8,128)S(1)} %get-tuple-element.29, bf16[4,10,512,576]{3,2,1,0:T(8,128)(2,1)} %bitcast.96, f32[4,10,128,512]{3,2,1,0:T(8,128)} %get-tuple-element.35, f32[4,10,128]{2,1,0:T(8,128)S(1)} %get-tuple-element.34, pred[4,10,512]{2,1,0:T(8,128)(4,1)S(1)} %copy.114), kind=kOutput, calls=%fused_computation.10 | convolution fusion | flops 2702704640 | bytes 36761600 | tf_op jit(solution)/shard_map/sbht,sbtc->sbhc/dot_general | solution.py:156
  365.1 2.7 broadcast_select_fusion.3
  367.8 2.1 gather_fusion.2
  369.9 3.7 broadcast_select_fusion.2
  373.6 6.0 %all-to-all-start.1 = ((bf16[128,64,128]{2,1,0:T(8,128)(2,1)}), bf16[128,64,128]{2,1,0:T(8,128)(2,1)}, u32[]{:S(2)}, u32[]{:S(2)}) async-start(bf16[128,64,128]{2,1,0:T(8,128)(2,1)} %broadcast_select_fusion.2), calls=%async_computation.1 | async-start | bytes 4194304 | tf_op jit(solution)/shard_map/all_to_all | solution.py:83
  379.7 54.5 %all_gather.9 = bf16[4,10,64,128]{3,0,1,2:T(4,128)(2,1)S(1)} all-gather(bf16[4,10,4,128]{3,0,1,2:T(4,128)(2,1)S(1)} %copy.106), channel_id=1, replica_groups=mesh['req'=8,'pos'=16] {'pos'}, dimensions={2}, use_global_device_ids=true | all-gather | bytes 696320 | tf_op jit(solution)/shard_map/all_gather | solution.py:99
  434.3 0.1 slice.42
  434.4 23.1 %all_gather.10 = bf16[4,10,64]{1,0,2:T(4,128)(2,1)S(1)} all-gather(bf16[4,10,4]{1,0,2:T(4,128)(2,1)S(1)} %copy.108), channel_id=1, replica_groups=mesh['req'=8,'pos'=16] {'pos'}, dimensions={2}, use_global_device_ids=true | all-gather | bytes 5440 | tf_op jit(solution)/shard_map/all_gather | solution.py:100
  457.6 0.1 copy.135
  457.8 0.6 gather_fusion.4
  458.5 0.1 copy.131
  458.6 0.6 dynamic-slice
  460.0 1.0 maximum_bitcast_fusion
  461.0 2.1 fusion.7
  463.2 2.3 gather_fusion.3
  465.6 0.7 maximum_bitcast_fusion.1
  466.3 1.5 fusion.15
  467.9 0.8 copy.127
  468.7 7.9 %copy.126 = bf16[4,1,1024,576]{2,3,1,0:T(8,128)(2,1)} copy(bf16[4,1,1024,576]{3,2,0,1:T(8,128)(2,1)} %bitcast.97) | data formatting | bytes 9437184
  476.6 0.2 copy.122
  476.8 73.5 %all-reduce.1 = bf16[4,10,128]{1,0,2:T(4,128)(2,1)S(1)} all-reduce(bf16[4,10,128]{1,0,2:T(4,128)(2,1)S(1)} %copy.122), channel_id=3, replica_groups=mesh['req'=8,'pos'=16] {'pos'}, use_global_device_ids=true, to_apply=%region_10.11.clone | all-reduce | flops 5120 | bytes 20480
  550.4 1.1 divide_convert_fusion
  551.6 1.6 fusion.23
  553.1 0.7 copy.128
  (64 shorter events, 1.8 us)
Async XLA Ops:
  7.2 452.9 %copy-start = (bf16[6,1,1024,128]{3,2,1,0:T(8,128)(2,1)S(1)}, bf16[6,1,1024,128]{3,2,1,0:T(8,128)(2,1)}, u32[]{:S(2)}) copy-start(bf16[6,1,1024,128]{3,2,1,0:T(8,128)(2,1)} %param.15) | copy-start | bytes 4718596
  45.6 11.7 %copy-start.3 = (bf16[4,10,8,64]{3,2,1,0:T(8,128)(2,1)S(1)}, bf16[4,10,8,64]{3,2,1,0:T(8,128)(2,1)}, u32[]{:S(2)}) copy-start(bf16[4,10,8,64]{3,2,1,0:T(8,128)(2,1)} %param.22) | copy-start | bytes 122884
  45.6 11.7 %copy-start.7 = (bf16[4,10,8,128]{3,2,1,0:T(8,128)(2,1)S(1)}, bf16[4,10,8,128]{3,2,1,0:T(8,128)(2,1)}, u32[]{:S(2)}) copy-start(bf16[4,10,8,128]{3,2,1,0:T(8,128)(2,1)} %param.21) | copy-start | bytes 245764
  45.6 14.5 %copy-start.4 = (s32[4,10,32]{2,0,1:T(4,128)S(1)}, s32[4,10,32]{2,0,1:T(4,128)}, u32[]{:S(2)}) copy-start(s32[4,10,32]{2,0,1:T(4,128)} %param.27) | copy-start | bytes 15364
  45.6 158.9 %all-to-all-start = ((bf16[128,64,576]{2,1,0:T(8,128)(2,1)}), bf16[128,64,576]{2,1,0:T(8,128)(2,1)}, u32[]{:S(2)}, u32[]{:S(2)}) async-start(bf16[128,64,576]{2,1,0:T(8,128)(2,1)} %broadcast_select_fusion), calls=%async_computation | async-start | bytes 20971520 | tf_op jit(solution)/shard_map/all_to_all | solution.py:76
  57.2 183.1 %all-gather.2.cloned.1.call-start = ((), (), s32[]{:S(2)}) async-start(), calls=%async_computation.2 | async-start | bytes 6963200 | tf_op jit(solution)/shard_map/all_gather | solution.py:146
  59.9 490.5 %all-reduce.4.cloned.1.call-start = ((), (), s32[]{:S(2)}) async-start(), calls=%async_computation.3 | async-start | bytes 10485760
  365.1 14.5 %copy-start.5 = (bf16[4,10,4,128]{3,2,1,0:T(4,128)(2,1)S(1)}, bf16[4,10,4,128]{3,2,1,0:T(4,128)(2,1)}, u32[]{:S(2)}) copy-start(bf16[4,10,4,128]{3,2,1,0:T(4,128)(2,1)} %param.25) | copy-start | bytes 122884
  367.8 66.7 %copy-start.6 = (bf16[4,10,4]{1,2,0:T(4,128)(2,1)S(1)}, bf16[4,10,4]{1,2,0:T(4,128)(2,1)}, u32[]{:S(2)}) copy-start(bf16[4,10,4]{1,2,0:T(4,128)(2,1)} %param.26) | copy-start | bytes 964
  367.8 90.0 %copy-start.1 = (s32[32]{0:T(128)S(1)}, s32[32]{0:T(128)}, u32[]{:S(2)}) copy-start(s32[32]{0:T(128)} %param.19) | copy-start | bytes 388
  367.8 90.8 %copy-start.9 = (u32[128]{0:T(128)S(1)}, u32[128]{0:T(128)}, u32[]{:S(2)}) copy-start(u32[128]{0:T(128)} %constant.153) | copy-start | bytes 1540
  367.8 92.0 %copy-start.8 = (s32[6]{0:T(128)S(1)}, s32[6]{0:T(128)}, u32[]{:S(2)}) copy-start(s32[6]{0:T(128)} %param.16) | copy-start | bytes 76
  373.6 89.6 %all-to-all-start.1 = ((bf16[128,64,128]{2,1,0:T(8,128)(2,1)}), bf16[128,64,128]{2,1,0:T(8,128)(2,1)}, u32[]{:S(2)}, u32[]{:S(2)}) async-start(bf16[128,64,128]{2,1,0:T(8,128)(2,1)} %broadcast_select_fusion.2), calls=%async_computation.1 | async-start | bytes 4194304 | tf_op jit(solution)/shard_map/all_to_all | solution.py:83
  465.6 11.1 %copy-start.2 = (bf16[4,16,64,128]{3,2,1,0:T(8,128)(2,1)}, bf16[4,16,64,128]{3,2,1,0:T(8,128)(2,1)S(1)}, u32[]{:S(2)}) copy-start(bf16[4,16,64,128]{3,2,1,0:T(8,128)(2,1)S(1)} %gather_fusion.3) | copy-start | bytes 3145732
Sparse Core Ops, SparseCore 0:
  60.8 149.6 all-gather.1
  365.2 132.9 all-reduce.3
where the time goes:
time: 562 us; the launch traced here: 561 us
  blocking collectives  234 us (42%)
  waiting for transfers between devices  118 us (21%)
  local copies, waits for them, and re-layouts  82.4 us (15%)
  other arithmetic  49.6 us (9%)
  matrix products  43.6 us (8%)
  starting transfers between devices  17.9 us (3%)
  between operations  15.1 us (3%)
    all_to_all x1, waiting for transfers between devices, body(): lax.all_to_all(send_latent.reshape(req_count * pos_count, -1, lat_width),...  118 us
    pmax x1, blocking collectives, body(): overall = lax.pmax(largest, 'pos')  83.2 us
    unnamed x1, blocking collectives  73.5 us
    all_gather x1, blocking collectives, body(): lax.all_gather(idx_query, 'pos', axis=2, tiled=True)  54.5 us
    gather x3, local copies, waits for them, and re-layouts, outgoing_pages(): routed = jnp.where(occupied[:, None, None], masked[chosen_rows], zero_value)  23.6 us
    all_gather x1, blocking collectives, body(): lax.all_gather(idx_weight, 'pos', axis=2, tiled=True)  23.1 us
    unnamed x29, local copies, waits for them, and re-layouts  20.3 us
    dot_general x1, matrix products, body(): jnp.einsum('sbhc,sbtc->sbht', lax.all_gather(queries, 'pos', axis=2, tile...  20.2 us
  transfers between devices with their start and end apart: 4, of which 1 were waited for; matrix products, arithmetic and copies ran while one was open for 16% of the time, Pallas kernels for 0%

commit v1 on v0

v1 whole, which is shorter than its diff:
```python
import jax
import jax.numpy as jnp
from jax import lax
from jax.experimental import pallas as pl
from jax.experimental.pallas import tpu as pltpu
from jax.sharding import PartitionSpec as P

KV, ROPE, NOPE, IDIM, PAGE = 512, 64, 128, 128, 64
LAT = KV + ROPE
STEPS, RES, NEW, BATCH, HEADS_DEV, IHEADS_DEV = 4, 6, 4, 10, 8, 4
CTX_DEV, PG_LOC, N_REQ, SIDE = 1024, 16, 8, 4
QW = 640
HALF = PAGE // 2
QROWS = STEPS * HEADS_DEV
IROWS = STEPS * IHEADS_DEV
BF, F32 = jnp.bfloat16, jnp.float32
MESH = pl.DeviceIdType.MESH
SCALE = (NOPE + ROPE) ** (-0.5)

CHUNKS = (
    [("idx", 0, 0), ("idx", 0, 1), ("rope", 0, 0)]
    + [("lat", j, h) for j in range(KV // 128) for h in range(2)]
)
N_CH = len(CHUNKS)
RING = 3
GROUPS = ((0, 6), (6, 2), (8, 2))


def kernel(
    chosen, sources, limits, lat, idx, rope, qown, iqown, reslat, residx, bias,
    out_lat, out_idx, out_is, out_latent, a_buf,
    b_bufs, zsend, zrecvs, q_all, iq_all, kbuf, ki_res, kfin, kifin, numer, stats,
    ra, rsa, nb_buf, stb, rb, rsb,
    sa_s, sa_r, sb_s, sb_r, sz_s, sz_r, own_a, own_b, load_sem, out_sem, kb_sem,
    ag_s, ag_r, rs_s, rs_r,
):
    req = lax.axis_index("req")
    pos = lax.axis_index("pos")
    y, x = pos // SIDE, pos % SIDE

    def along(axis, delta):
        if axis == 0:
            return (req, y * SIDE + (x + delta) % SIDE)
        return (req, ((y + delta) % SIDE) * SIDE + x)

    def mine(axis):
        return x if axis == 0 else y

    def remote(src, dst, send, recv, target):
        return pltpu.make_async_remote_copy(
            src_ref=src, dst_ref=dst, send_sem=send, recv_sem=recv,
            device_id=target, device_id_type=MESH,
        )

    barrier = pltpu.get_barrier_semaphore()
    for delta in range(1, N_REQ):
        pl.semaphore_signal(barrier, 1, device_id=((req + delta) % N_REQ, pos), device_id_type=MESH)
    for axis in range(2):
        for delta in range(1, SIDE):
            pl.semaphore_signal(barrier, 1, device_id=along(axis, delta), device_id_type=MESH)
    pl.semaphore_wait(barrier, N_REQ - 1 + 2 * (SIDE - 1))

    def first_axis(i):
        return i % 2

    def chunk_source(i, coord):
        kind, plane, half = CHUNKS[i]
        if kind == "rope":
            ref, rows, lanes = rope, pl.ds(0, HALF), pl.ds(0, 128)
        elif kind == "idx":
            ref, rows, lanes = idx, pl.ds(half * HALF, HALF), pl.ds(0, 128)
        else:
            ref, rows, lanes = lat, pl.ds(half * HALF, HALF), pl.ds(plane * 128, 128)
        if first_axis(i) == 0:
            return ref.at[:, :, coord, rows, lanes]
        return ref.at[:, coord, :, rows, lanes]

    def copies_a(i):
        axis = first_axis(i)
        return [
            remote(
                chunk_source(i, (mine(axis) + delta) % SIDE), a_buf.at[i, mine(axis)],
                sa_s.at[i, delta - 1], sa_r.at[i, delta - 1], along(axis, delta),
            )
            for delta in range(1, SIDE)
        ]

    def own_copy_a(i):
        coord = mine(first_axis(i))
        return pltpu.make_async_copy(chunk_source(i, coord), a_buf.at[i, coord], own_a.at[i])

    def copies_b(i):
        axis = 1 - first_axis(i)
        return [
            remote(
                a_buf.at[i, :, :, (mine(axis) + delta) % SIDE], b_bufs[i].at[mine(axis)],
                sb_s.at[i, delta - 1], sb_r.at[i, delta - 1], along(axis, delta),
            )
            for delta in range(1, SIDE)
        ]

    def own_copy_b(i):
        coord = mine(1 - first_axis(i))
        return pltpu.make_async_copy(a_buf.at[i, :, :, coord], b_bufs[i].at[coord], own_b.at[i])

    def copy_z(i, delta):
        return remote(
            zsend.at[i % RING, delta - 1], zrecvs[i].at[req],
            sz_s.at[i, delta - 1], sz_r.at[i, delta - 1], ((req + delta) % N_REQ, pos),
        )

    def start_a(i):
        for copy in copies_a(i):
            copy.start()

    def a_to_b(i):
        own_copy_a(i).wait()
        for copy in copies_a(i):
            copy.wait_recv()
        for copy in copies_b(i):
            copy.start()
        own_copy_b(i).start()

    def b_to_z(i):
        own_copy_b(i).wait()
        for copy in copies_b(i):
            copy.wait_recv()
        if i >= RING:
            for delta in range(1, N_REQ):
                copy_z(i - RING, delta).wait_send()

        def stage(delta, carry):
            k = chosen[(req + delta) % N_REQ]
            zsend[i % RING, delta - 1] = b_bufs[i][:, :, k]
            copy_z(i, delta).start()
            return carry

        lax.fori_loop(1, N_REQ, stage, 0)
        zrecvs[i][req] = b_bufs[i][:, :, chosen[req]]

    def wait_z(i):
        for delta in range(1, N_REQ):
            copy_z(i, delta).wait_recv()

    def out_copies(kind):
        if kind == "idx":
            return pltpu.make_async_copy(kifin, out_idx, out_sem.at[0])
        return pltpu.make_async_copy(kfin, out_lat, out_sem.at[1])

    def finalize(i):
        kind, plane, half = CHUNKS[i]
        by_x = first_axis(i) == 0

        def page(n, carry):
            outer, inner = n // SIDE, n % SIDE
            l = outer * SIDE + inner if by_x else inner * SIDE + outer
            base = (l * (SIDE * SIDE) + pos) * PAGE
            row = lax.broadcasted_iota(jnp.int32, (HALF, 128), 0)
            for k in range(NEW):
                tile = zrecvs[i][sources[k], outer, inner]
                if kind == "rope":
                    for part in range(2):
                        keep = row[:, :ROPE] + (base + part * HALF) < limits[k]
                        value = tile[:, part * ROPE : (part + 1) * ROPE].astype(F32)
                        kfin[k, l, part * HALF : (part + 1) * HALF, KV:LAT] = jnp.where(
                            keep, value, 0.0
                        ).astype(BF)
                else:
                    keep = row + (base + half * HALF) < limits[k]
                    value = jnp.where(keep, tile.astype(F32), 0.0).astype(BF)
                    rows = slice(half * HALF, (half + 1) * HALF)
                    if kind == "idx":
                        kifin[k, l, rows, :] = value
                    else:
                        kfin[k, l, rows, plane * 128 : (plane + 1) * 128] = value
            return carry

        lax.fori_loop(0, SIDE * SIDE, page, 0)

    spans = (pl.ds(0, BATCH // 2), pl.ds(BATCH // 2, BATCH // 2))

    def gather_copies(phase):
        copies = []
        for way in range(2):
            axis = way if phase == 0 else 1 - way
            for which, (own, every) in enumerate(((qown, q_all), (iqown, iq_all))):
                for delta in range(1, SIDE):
                    if phase == 0:
                        src, dst = own.at[spans[way]], every.at[y, x, spans[way]]
                    elif way == 0:
                        src = dst = every.at[y, :, spans[way]]
                    else:
                        src = dst = every.at[:, x, spans[way]]
                    at = (phase, way, which, delta - 1)
                    copies.append(remote(src, dst, ag_s.at[at], ag_r.at[at], along(axis, delta)))
        return copies

    own_q = pltpu.make_async_copy(qown, q_all.at[y, x], load_sem.at[0])
    own_iq = pltpu.make_async_copy(iqown, iq_all.at[y, x], load_sem.at[1])
    load_ki = pltpu.make_async_copy(residx, ki_res, load_sem.at[2])

    def load_k(b):
        return pltpu.make_async_copy(reslat.at[b], kbuf.at[b % 2], kb_sem.at[b])

    def attend(b, g, keys, flipped):
        def part(n, carry):
            q = q_all[pl.ds(2 * n, 2), :, b, :, 0:LAT].reshape(2 * SIDE * QROWS, LAT)
            k = keys()
            key_dim = 0 if flipped else 1
            s = lax.dot_general(q, k, (((1,), (key_dim,)), ((), ())), preferred_element_type=F32)
            s = (s * SCALE).reshape(2 * SIDE, QROWS, CTX_DEV) + bias[b][None]
            s = s.reshape(2 * SIDE * QROWS, CTX_DEV)
            top = jnp.maximum(jnp.max(s, axis=1, keepdims=True), -1e29)
            e = jnp.exp(s - top)
            total = jnp.sum(e, axis=1, keepdims=True)
            v = k[:KV] if flipped else k[:, :KV]
            o = lax.dot_general(
                e.astype(BF), v, (((1,), (1 - key_dim,)), ((), ())), preferred_element_type=F32
            )
            numer[pl.ds(2 * n, 2), :, b] = o.astype(BF).reshape(2, SIDE, QROWS, KV)
            lane = lax.broadcasted_iota(jnp.int32, (2 * SIDE * QROWS, 128), 1)
            shape = (2, SIDE, QROWS, 128)
            here = (lane == b - GROUPS[g][0])
            old_top = stats[g, 0, pl.ds(2 * n, 2)].reshape(2 * SIDE * QROWS, 128)
            old_sum = stats[g, 1, pl.ds(2 * n, 2)].reshape(2 * SIDE * QROWS, 128)
            stats[g, 0, pl.ds(2 * n, 2)] = jnp.where(here, top, old_top).reshape(shape)
            stats[g, 1, pl.ds(2 * n, 2)] = jnp.where(here, total, old_sum).reshape(shape)
            return carry

        lax.fori_loop(0, 2, part, 0)

    def index_scores(b, keys):
        def part(n, carry):
            block = iq_all[:, :, b].reshape(SIDE * SIDE * IROWS, 2 * IDIM)
            k = keys(n)
            logits = lax.dot_general(
                block[:, :IDIM], k, (((1,), (1,)), ((), ())), preferred_element_type=F32
            )
            weight = block[:, IDIM : IDIM + 1].astype(F32)
            value = jnp.maximum(logits, 0.0) * weight
            cols = pl.ds(pl.multiple_of(n * 256, 256), 256)
            out_is[b, :, cols] = jnp.sum(value.reshape(SIDE * SIDE, IROWS, 256), axis=0)
            return carry

        lax.fori_loop(0, CTX_DEV // 256, part, 0)

    def attend_res(b):
        load_k(b).wait()
        attend(b, 0, lambda: kbuf[b % 2], True)
        if b + 2 < RES:
            load_k(b + 2).start()

    def attend_new(k, g):
        attend(RES + k, g, lambda: kfin[k].reshape(CTX_DEV, LAT), False)

    def index_res(b):
        index_scores(b, lambda n: ki_res[b, pl.ds(pl.multiple_of(n * 256, 256), 256)])

    def index_new(k):
        index_scores(RES + k, lambda n: kifin[k, pl.ds(n * 4, 4)].reshape(256, IDIM))

    def lanes(way):
        return pl.ds(way * 256, 256)

    def reduce_copies(g, phase, way):
        b0, count = GROUPS[g]
        span = pl.ds(b0, count)
        axis = way if phase == 0 else 1 - way
        copies = []
        for delta in range(1, SIDE):
            other = (mine(axis) + delta) % SIDE
            if phase == 0:
                if way == 0:
                    src, src_st = numer.at[:, other, span, :, lanes(way)], stats.at[g, :, :, other]
                else:
                    src, src_st = numer.at[other, :, span, :, lanes(way)], stats.at[g, :, other]
                dst, dst_st = ra.at[way, delta - 1, :, span], rsa.at[g, way, delta - 1]
            else:
                src, src_st = nb_buf.at[way, other, span], stb.at[g, way, other]
                dst, dst_st = rb.at[way, delta - 1, span], rsb.at[g, way, delta - 1]
            target = along(axis, delta)
            for which, (s, d) in enumerate(((src, dst), (src_st, dst_st))):
                at = (g, phase, way, which, delta - 1)
                copies.append(remote(s, d, rs_s.at[at], rs_r.at[at], target))
        return copies

    def start_reduce(g, phase, way):
        for copy in reduce_copies(g, phase, way):
            copy.start()

    def merged(tops, sums):
        top = tops[0]
        for value in tops[1:]:
            top = jnp.maximum(top, value)
        factors = [jnp.exp(value - top) for value in tops]
        total = factors[0] * sums[0]
        for factor, value in zip(factors[1:], sums[1:]):
            total = total + factor * value
        return top, factors, total

    def combine_a(g, way):
        b0, count = GROUPS[g]
        for copy in reduce_copies(g, 0, way):
            copy.wait_recv()

        def block(j, carry):
            if way == 0:
                own = (stats[g, 0, j, x], stats[g, 1, j, x])
            else:
                own = (stats[g, 0, y, j], stats[g, 1, y, j])
            tops = [own[0]] + [rsa[g, way, d, 0, j] for d in range(SIDE - 1)]
            sums = [own[1]] + [rsa[g, way, d, 1, j] for d in range(SIDE - 1)]
            top, factors, total = merged(tops, sums)
            stb[g, way, j, 0] = top
            stb[g, way, j, 1] = total
            for n in range(count):
                if way == 0:
                    first = numer[j, x, b0 + n, :, 0:256]
                else:
                    first = numer[y, j, b0 + n, :, 256:512]
                acc = first.astype(F32) * factors[0][:, n : n + 1]
                for d in range(SIDE - 1):
                    acc = acc + ra[way, d, j, b0 + n].astype(F32) * factors[d + 1][:, n : n + 1]
                nb_buf[way, j, b0 + n] = acc.astype(BF)
            return carry

        lax.fori_loop(0, SIDE, block, 0)
        start_reduce(g, 1, way)

    def combine_b(g, way):
        b0, count = GROUPS[g]
        for copy in reduce_copies(g, 1, way):
            copy.wait_recv()
        here = mine(1 - way)
        tops = [stb[g, way, here, 0]] + [rsb[g, way, d, 0] for d in range(SIDE - 1)]
        sums = [stb[g, way, here, 1]] + [rsb[g, way, d, 1] for d in range(SIDE - 1)]
        top, factors, total = merged(tops, sums)
        for n in range(count):
            acc = nb_buf[way, here, b0 + n].astype(F32) * factors[0][:, n : n + 1]
            for d in range(SIDE - 1):
                acc = acc + rb[way, d, b0 + n].astype(F32) * factors[d + 1][:, n : n + 1]
            out_latent[b0 + n, :, way * 256 : (way + 1) * 256] = (
                acc / total[:, n : n + 1]
            ).astype(BF)

    own_q.start()
    own_iq.start()
    for i in range(2):
        own_copy_a(i).start()
        start_a(i)
    for copy in gather_copies(0):
        copy.start()
    for i in range(2, 5):
        own_copy_a(i).start()
        start_a(i)
    load_ki.start()
    load_k(0).start()
    load_k(1).start()
    stats[...] = jnp.zeros_like(stats)
    a_to_b(0)
    a_to_b(1)
    b_to_z(0)
    own_q.wait()
    own_iq.wait()
    for copy in gather_copies(0):
        copy.wait_recv()
    for copy in gather_copies(1):
        copy.start()
    b_to_z(1)
    a_to_b(2)

    for i in range(N_CH):
        wait_z(i)
        if i + 2 < N_CH:
            b_to_z(i + 2)
        if i + 3 < N_CH:
            a_to_b(i + 3)
        if i + 5 < N_CH:
            own_copy_a(i + 5).start()
            start_a(i + 5)
        finalize(i)
        if i == 1:
            out_copies("idx").start()
        if i == 3:
            for copy in gather_copies(1):
                copy.wait_recv()
            attend_res(0)
        elif i == 4:
            attend_res(1)
            attend_res(2)
            attend_res(3)
        elif i == 5:
            attend_res(4)
            attend_res(5)
            for way in range(2):
                start_reduce(0, 0, way)
            load_ki.wait()
            index_res(0)
            index_res(1)
        elif i == 6:
            for b in range(2, RES):
                index_res(b)
        elif i == 7:
            for way in range(2):
                combine_a(0, way)
            index_new(0)
            index_new(1)
        elif i == 8:
            index_new(2)
            index_new(3)
        elif i == 9:
            for way in range(2):
                combine_b(0, way)
    out_copies("lat").start()
    attend_new(0, 1)
    attend_new(1, 1)
    for way in range(2):
        start_reduce(1, 0, way)
    attend_new(2, 2)
    attend_new(3, 2)
    for way in range(2):
        start_reduce(2, 0, way)
    for g in (1, 2):
        for way in range(2):
            combine_a(g, way)
    for g in (1, 2):
        for way in range(2):
            combine_b(g, way)

    for i in range(N_CH):
        for copy in copies_a(i) + copies_b(i):
            copy.wait_send()
    for i in range(N_CH - RING, N_CH):
        for delta in range(1, N_REQ):
            copy_z(i, delta).wait_send()
    for phase in range(2):
        for copy in gather_copies(phase):
            copy.wait_send()
        for g in range(len(GROUPS)):
            for way in range(2):
                for copy in reduce_copies(g, phase, way):
                    copy.wait_send()
    out_copies("idx").wait()
    out_copies("lat").wait()


def run_kernel(*operands):
    smem = pl.BlockSpec(memory_space=pltpu.SMEM)
    vmem = pl.BlockSpec(memory_space=pltpu.VMEM)
    hbm = pl.BlockSpec(memory_space=pl.ANY)
    dma = pltpu.SemaphoreType.DMA
    n_groups = len(GROUPS)
    tile = (SIDE, SIDE, HALF, 128)
    return pl.pallas_call(
        kernel,
        out_shape=(
            jax.ShapeDtypeStruct((NEW, PG_LOC, PAGE, LAT), BF),
            jax.ShapeDtypeStruct((NEW, PG_LOC, PAGE, IDIM), BF),
            jax.ShapeDtypeStruct((BATCH, IROWS, CTX_DEV), F32),
            jax.ShapeDtypeStruct((BATCH, QROWS, KV), BF),
            jax.ShapeDtypeStruct((N_CH, SIDE, NEW, SIDE, HALF, 128), BF),
        ),
        in_specs=[smem] * 3 + [hbm] * 7 + [vmem],
        out_specs=(hbm, hbm, vmem, vmem, hbm),
        scratch_shapes=[
            (pltpu.VMEM((SIDE, SIDE, NEW, HALF, 128), BF),) * N_CH,
            pltpu.VMEM((RING, N_REQ - 1) + tile, BF),
            (pltpu.VMEM((N_REQ,) + tile, BF),) * N_CH,
            pltpu.VMEM((SIDE, SIDE, BATCH, QROWS, QW), BF),
            pltpu.VMEM((SIDE, SIDE, BATCH, IROWS, 2 * IDIM), BF),
            pltpu.VMEM((2, LAT, CTX_DEV), BF),
            pltpu.VMEM((RES, CTX_DEV, IDIM), BF),
            pltpu.VMEM((NEW, PG_LOC, PAGE, LAT), BF),
            pltpu.VMEM((NEW, PG_LOC, PAGE, IDIM), BF),
            pltpu.VMEM((SIDE, SIDE, BATCH, QROWS, KV), BF),
            pltpu.VMEM((n_groups, 2, SIDE, SIDE, QROWS, 128), F32),
            pltpu.VMEM((2, SIDE - 1, SIDE, BATCH, QROWS, 256), BF),
            pltpu.VMEM((n_groups, 2, SIDE - 1, 2, SIDE, QROWS, 128), F32),
            pltpu.VMEM((2, SIDE, BATCH, QROWS, 256), BF),
            pltpu.VMEM((n_groups, 2, SIDE, 2, QROWS, 128), F32),
            pltpu.VMEM((2, SIDE - 1, BATCH, QROWS, 256), BF),
            pltpu.VMEM((n_groups, 2, SIDE - 1, 2, QROWS, 128), F32),
            dma((N_CH, 3)), dma((N_CH, 3)), dma((N_CH, 3)), dma((N_CH, 3)),
            dma((N_CH, N_REQ - 1)), dma((N_CH, N_REQ - 1)),
            dma((N_CH,)), dma((N_CH,)), dma((3,)), dma((2,)), dma((RES,)),
            dma((2, 2, 2, 3)), dma((2, 2, 2, 3)),
            dma((n_groups, 2, 2, 2, 3)), dma((n_groups, 2, 2, 2, 3)),
        ],
        compiler_params=pltpu.CompilerParams(
            collective_id=0, has_side_effects=True, vmem_limit_bytes=63 * 2**20
        ),
        name="decode_step",
    )(*operands)


def body(
    res_latent, res_index, res_len, arrive_latent, arrive_index, arrive_len, destination,
    q_nope, q_rope, w_uk, w_uv, idx_query, idx_weight, selected,
):
    req_index = lax.axis_index("req")
    pos_index = lax.axis_index("pos")
    routing = destination.reshape(N_REQ, NEW)
    group_ids = jnp.arange(N_REQ, dtype=jnp.int32)
    arrival_ids = jnp.arange(NEW, dtype=jnp.int32)
    matches = routing[req_index][None, :] == group_ids[:, None]
    chosen = jnp.sum(jnp.where(matches, arrival_ids[None, :], 0), axis=1)
    sources = jnp.sum(jnp.where(routing == req_index, group_ids[:, None], 0), axis=0)
    new_lengths = arrive_len[sources * NEW + arrival_ids]

    paged = arrive_latent.reshape(NEW, SIDE, SIDE, PAGE, LAT)
    rope = jnp.concatenate([paged[..., :HALF, KV:], paged[..., HALF:, KV:]], axis=-1)

    absorbed = jnp.einsum("sbhn,hnc->sbhc", q_nope, w_uk, preferred_element_type=F32).astype(BF)
    pad = jnp.zeros(q_rope.shape[:-1] + (QW - LAT,), BF)
    queries = jnp.concatenate([absorbed, q_rope, pad], axis=-1)
    queries = queries.transpose(1, 0, 2, 3).reshape(BATCH, QROWS, QW)
    spread = jnp.broadcast_to(idx_weight[..., None], idx_query.shape)
    idx_queries = jnp.concatenate([idx_query, spread], axis=-1)
    idx_queries = idx_queries.transpose(1, 0, 2, 3).reshape(BATCH, IROWS, 2 * IDIM)

    here = (selected % (SIDE * SIDE) == pos_index)[..., None]
    slots = jnp.arange(PG_LOC, dtype=jnp.int32)
    live = jnp.any(here & (selected[..., None] // (SIDE * SIDE) == slots), axis=2)
    bias = jnp.where(jnp.repeat(live, PAGE, axis=-1), 0.0, -1e30).astype(F32)
    bias = jnp.broadcast_to(
        bias.transpose(1, 0, 2)[:, :, None, :], (BATCH, STEPS, HEADS_DEV, CTX_DEV)
    ).reshape(BATCH, QROWS, CTX_DEV)

    new_latent, new_index, raw, latent, _ = run_kernel(
        chosen.astype(jnp.int32), sources.astype(jnp.int32), new_lengths,
        paged, arrive_index.reshape(NEW, SIDE, SIDE, PAGE, IDIM), rope,
        queries, idx_queries, res_latent[:, 0].transpose(0, 2, 1), res_index[:, 0], bias,
    )

    scored = jnp.sum(raw.reshape(BATCH, STEPS, IHEADS_DEV, CTX_DEV), axis=2) * IDIM ** (-0.5)
    lengths = jnp.concatenate([res_len, new_lengths])
    offsets = jnp.arange(CTX_DEV, dtype=jnp.int32)
    logical = (offsets // PAGE * (SIDE * SIDE) + pos_index) * PAGE + offsets % PAGE
    index_scores = jnp.where(logical[None, None, :] < lengths[:, None, None], scored, 0.0)
    index_scores = index_scores.transpose(1, 0, 2)[:, :, None, :]

    latent = latent.reshape(BATCH, STEPS, HEADS_DEV, KV)
    head_out = jnp.einsum("bshc,hcd->sbhd", latent, w_uv, preferred_element_type=F32).astype(BF)
    return (
        new_latent.reshape(NEW, 1, CTX_DEV, LAT),
        new_index.reshape(NEW, 1, CTX_DEV, IDIM),
        index_scores,
        head_out,
    )


def solution(mesh):
    placed = (
        P("req", "pos", None, None),
        P("req", "pos", None, None),
        P("req"),
        P("req", "pos", None),
        P("req", "pos", None),
        P(),
        P(),
        P(None, "req", "pos", None),
        P(None, "req", "pos", None),
        P("pos", None, None),
        P("pos", None, None),
        P(None, "req", "pos", None),
        P(None, "req", "pos"),
        P(None, "req", None),
    )
    return jax.shard_map(
        body,
        mesh=mesh,
        in_specs=placed,
        out_specs=(
            P("req", "pos", None, None),
            P("req", "pos", None, None),
            P(None, "req", "pos", None),
            P(None, "req", "pos", None),
        ),
        check_vma=False,
    )
```

time: 562 us -> 271 us (0.48)
  Pallas kernels: 0 us -> 236 us
  blocking collectives: 234 us -> 0 us
  waiting for transfers between devices: 118 us -> 0 us
  local copies, waits for them, and re-layouts: 82.4 us -> 26.9 us
  other arithmetic: 49.6 us -> 3.44 us
  matrix products: 43.6 us -> 0.7 us
  starting transfers between devices: 17.9 us -> 0 us
  between operations: 15.1 us -> 0.88 us
    pallas_call x0 -> x1, Pallas kernels: none -> 236 us  [run_kernel(): pl.pallas_call(kernel, out_shape=(jax.ShapeDtypeStruct((NEW, PG_LOC, PAGE...]
    all_to_all x2 -> x0, waiting for transfers between devices: 118 us -> none  [the longest x1 118 us: body(): lax.all_to_all(send_latent.reshape(req_count * pos_count, -1, lat_width),...]
    pmax x1 -> x0, blocking collectives: 83.2 us -> none  [body(): overall = lax.pmax(largest, 'pos')]
    all_gather x2 -> x0, blocking collectives: 77.6 us -> none  [the longest x1 54.5 us: body(): lax.all_gather(idx_query, 'pos', axis=2, tiled=True)]
    unnamed x1 -> x0, blocking collectives: 73.5 us -> none
    gather x8 -> x1, local copies, waits for them, and re-layouts: 58.1 us -> 1.83 us  [body(): new_lengths = arrive_len[sources * NEW + arrival_ids]]
    dot_general x8 -> x2, matrix products: 43.6 us -> 0.7 us  [the longest x1 0.41 us: body(): jnp.einsum('bshc,hcd->sbhd', latent, w_uv, preferred_element_type=F32)]
    select_n x8 -> x3, other arithmetic: 21.3 us -> 0.04 us  [the longest x1 0.03 us: body(): selected[..., None] // (SIDE * SIDE) == slots]
  transfers between devices with their start and end apart: 4 -> 0, of which waited for: 1 -> 0; matrix products, arithmetic and copies ran while one was open for 16% -> 0% of each run, Pallas kernels for 0% -> 0%
where the time goes in v1:
time: 271 us; the launch traced here: 268 us
  Pallas kernels  236 us (87%)
  local copies, waits for them, and re-layouts  26.9 us (10%)
  other arithmetic  3.44 us (1%)
    pallas_call x1, Pallas kernels, run_kernel(): pl.pallas_call(kernel, out_shape=(jax.ShapeDtypeStruct((NEW, PG_LOC, PAGE...  236 us
    unnamed x31, local copies, waits for them, and re-layouts  18.2 us

profile of v1, /device:TPU:0, one launch (start us, length us, event | category | flops | bytes accessed | tf_op | source)
XLA Modules:
  0.0 268.2 jit_solution(17255136101495060313)
XLA Ops:
  0.6 0.0 copy-start
  0.7 0.8 reshape.142
  1.4 0.6 select_reduce_fusion
  2.1 0.0 copy-start.8
  2.1 1.8 gather_fusion
  3.9 7.7 %copy.43 = bf16[4,1024,576]{2,1,0:T(8,128)(2,1)} copy(bf16[4,1024,576]{1,2,0:T(8,128)(2,1)} %param.17) | data formatting | bytes 9437184 | tf_op args[3]
  11.6 0.0 copy-done.8
  11.6 0.0 copy-start.5
  11.6 1.3 fusion.22
  12.9 1.1 pad_maximum_fusion.rope
  14.0 0.0 copy-done.5
  14.1 0.8 fusion.6
  14.9 0.1 broadcast_in_dim.76
  15.1 0.2 select_n.76
  15.2 0.0 copy-start.4
  15.2 1.2 broadcast_bitcast_fusion.bias
  16.5 0.0 copy-done
  16.5 0.0 copy-done.10
  16.5 0.3 fusion
  16.8 0.0 copy-done.4
  16.8 0.0 copy-start.7
  16.8 0.0 copy-start.6
  16.8 0.1 pad.6.clone
  16.9 0.2 maximum_bitcast_fusion
  17.1 1.0 copy.64
  18.1 0.0 copy-done.7
  18.1 0.1 copy.47
  18.2 0.1 broadcast_in_dim.73
  18.3 0.0 copy-done.6
  18.4 0.7 reshape.146.iqown
  19.1 236.3 %decode_step.1 = (bf16[4,16,64,576]{3,2,1,0:T(8,128)(2,1)}, bf16[4,16,64,128]{3,2,1,0:T(8,128)(2,1)}, f32[10,16,1024]{2,1,0:T(8,128)}, bf16[10,32,512]{2,1,0:T(8,128)(2,1)}, bf16[11,4,4,4,32,128]{5,4,3,2,1,0:T(8,128)(2,1)}) custom-call(s32[8]{0:T(128)} %get-tuple-element.27.chosen, s32[4]{0:T(128)} %copy-done.8, s32[4]{0:T(128)} %gather_fusion, ...), custom_call_target="tpu_custom_call" | custom-call | tf_op jit(solution)/shard_map/decode_step/pallas_call | solution.py:454
  255.4 0.0 copy-start.9
  255.4 0.0 copy-start.11
  255.4 1.3 reshape.150
  256.7 0.4 reduce_sum.29
  257.1 0.0 copy-done.9
  257.1 0.0 copy-done.11
  257.1 0.1 pad_add_fusion
  257.2 0.1 broadcast_compare_fusion
  257.3 0.1 select_bitcast_fusion
  257.4 0.8 copy.55
  258.2 7.7 %copy.53 = bf16[4,1,1024,576]{2,3,1,0:T(8,128)(2,1)} copy(bf16[4,1,1024,576]{3,2,0,1:T(8,128)(2,1)} %bitcast.54) | data formatting | bytes 9437184
  266.0 0.0 copy-done.2
  266.0 0.0 copy-done.3
  266.0 0.4 fusion.1
  266.4 0.7 copy.56
  267.1 0.1 copy-done.1
  267.2 1.0 copy.66
  (18 shorter events, 0.2 us)
Async XLA Ops:
  0.6 15.8 %copy-start = (bf16[4,10,8,128]{3,2,1,0:T(8,128)(2,1)S(1)}, bf16[4,10,8,128]{3,2,1,0:T(8,128)(2,1)}, u32[]{:S(2)}) copy-start(bf16[4,10,8,128]{3,2,1,0:T(8,128)(2,1)} %param.21) | copy-start | bytes 245764
  2.1 9.5 %copy-start.8 = (s32[4]{0:T(128)}, s32[4]{0:T(128)S(1)}, u32[]{:S(2)}) copy-start(s32[4]{0:T(128)S(1)} %get-tuple-element.26.sources) | copy-start | bytes 52
  11.6 2.4 copy-start.5
  14.0 2.5 copy-start.10
  15.2 1.5 copy-start.4
  16.8 1.3 copy-start.7
  16.8 1.5 copy-start.6
  255.4 1.7 copy-start.9
  255.4 1.7 copy-start.11
  258.2 7.7 %copy-start.2 = (bf16[8,512,128]{2,1,0:T(8,128)(2,1)S(1)}, bf16[8,512,128]{2,1,0:T(8,128)(2,1)}, u32[]{:S(2)}) copy-start(bf16[8,512,128]{2,1,0:T(8,128)(2,1)} %param.24) | copy-start | bytes 3145732
  258.2 7.7 %copy-start.3 = (bf16[10,32,512]{2,1,0:T(8,128)(2,1)S(1)}, bf16[10,32,512]{2,1,0:T(8,128)(2,1)}, u32[]{:S(2)}) copy-start(bf16[10,32,512]{2,1,0:T(8,128)(2,1)} %get-tuple-element.11) | copy-start | bytes 983044
  266.0 1.2 copy-start.1

commit v2 on v1

--- a/solution.py
+++ b/solution.py
@@ -7,12 +7,11 @@
 
 KV, ROPE, NOPE, IDIM, PAGE = 512, 64, 128, 128, 64
 LAT = KV + ROPE
-STEPS, RES, NEW, BATCH, HEADS_DEV, IHEADS_DEV = 4, 6, 4, 10, 8, 4
+STEPS, RES, NEW, BATCH, HEADS_DEV = 4, 6, 4, 10, 8
 CTX_DEV, PG_LOC, N_REQ, SIDE = 1024, 16, 8, 4
 QW = 640
 HALF = PAGE // 2
 QROWS = STEPS * HEADS_DEV
-IROWS = STEPS * IHEADS_DEV
 BF, F32 = jnp.bfloat16, jnp.float32
 MESH = pl.DeviceIdType.MESH
 SCALE = (NOPE + ROPE) ** (-0.5)
@@ -24,15 +23,16 @@
 N_CH = len(CHUNKS)
 RING = 3
 GROUPS = ((0, 6), (6, 2), (8, 2))
+STAT_ROWS = (16, 8, 8)
 
 
 def kernel(
-    chosen, sources, limits, lat, idx, rope, qown, iqown, reslat, residx, bias,
+    chosen, sources, limits, lat, idx, rope, qown, wown, reslat, residx, bias,
     out_lat, out_idx, out_is, out_latent, a_buf,
-    b_bufs, zsend, zrecvs, q_all, iq_all, kbuf, ki_res, kfin, kifin, numer, stats,
-    ra, rsa, nb_buf, stb, rb, rsb,
+    b_bufs, zsend, zrecvs, q_all, w_all, iq_buf, kbuf, ki_res, kfin, kifin, numer, stats,
+    ra, rsa, nb_buf, stb, rb, rsb, fbuf,
     sa_s, sa_r, sb_s, sb_r, sz_s, sz_r, own_a, own_b, load_sem, out_sem, kb_sem,
-    ag_s, ag_r, rs_s, rs_r,
+    ag_s, ag_r, aw_s, aw_r, rs_s, rs_r,
 ):
     req = lax.axis_index("req")
     pos = lax.axis_index("pos")
@@ -179,30 +179,75 @@
 
     spans = (pl.ds(0, BATCH // 2), pl.ds(BATCH // 2, BATCH // 2))
 
-    def gather_copies(phase):
+    def gather_views(phase, way):
+        if phase == 0:
+            return (qown.at[spans[way]], q_all.at[y, x, spans[way]])
+        if way == 0:
+            block = q_all.at[y, :, spans[way]]
+        else:
+            block = q_all.at[:, x, spans[way]]
+        return (block, block)
+
+    def gather_near(phase):
         copies = []
         for way in range(2):
             axis = way if phase == 0 else 1 - way
-            for which, (own, every) in enumerate(((qown, q_all), (iqown, iq_all))):
-                for delta in range(1, SIDE):
-                    if phase == 0:
-                        src, dst = own.at[spans[way]], every.at[y, x, spans[way]]
-                    elif way == 0:
-                        src = dst = every.at[y, :, spans[way]]
-                    else:
-                        src = dst = every.at[:, x, spans[way]]
-                    at = (phase, way, which, delta - 1)
-                    copies.append(remote(src, dst, ag_s.at[at], ag_r.at[at], along(axis, delta)))
+            src, dst = gather_views(phase, way)
+            for n, delta in enumerate((1, SIDE - 1)):
+                at = (phase, way, 0, n)
+                copies.append(remote(src, dst, ag_s.at[at], ag_r.at[at], along(axis, delta)))
         return copies
 
+    def gather_far(phase):
+        copies = []
+        for way in range(2):
+            axis = way if phase == 0 else 1 - way
+            for n, delta in enumerate((1, SIDE - 1)):
+                rows = pl.ds(n * (QROWS // 2), QROWS // 2)
+                fx = (x - delta) % SIDE if axis == 0 else x
+                fy = (y - delta) % SIDE if axis == 1 else y
+                if phase == 0:
+                    block = q_all.at[fy, fx, spans[way], rows]
+                elif way == 0:
+                    block = q_all.at[fy, :, spans[way], rows]
+                else:
+                    block = q_all.at[:, fx, spans[way], rows]
+                at = (phase, way, 1, n)
+                copies.append(remote(block, block, ag_s.at[at], ag_r.at[at], along(axis, delta)))
+        return copies
+
+    def weight_copies(phase):
+        axis = phase
+        block = w_all.at[y, x] if phase == 0 else w_all.at[y]
+        return [
+            remote(
+                wown if phase == 0 else block, block, aw_s.at[phase, delta - 1],
+                aw_r.at[phase, delta - 1], along(axis, delta),
+            )
+            for delta in range(1, SIDE)
+        ]
+
     own_q = pltpu.make_async_copy(qown, q_all.at[y, x], load_sem.at[0])
-    own_iq = pltpu.make_async_copy(iqown, iq_all.at[y, x], load_sem.at[1])
+    own_w = pltpu.make_async_copy(wown, w_all.at[y, x], load_sem.at[1])
     load_ki = pltpu.make_async_copy(residx, ki_res, load_sem.at[2])
 
     def load_k(b):
         return pltpu.make_async_copy(reslat.at[b], kbuf.at[b % 2], kb_sem.at[b])
 
+    def as_row(column):
+        size = column.shape[0]
+        row = lax.broadcasted_iota(jnp.int32, (size, size), 0)
+        lane = lax.broadcasted_iota(jnp.int32, (size, size), 1)
+        return jnp.sum(jnp.where(row == lane, column, 0.0), axis=0, keepdims=True)
+
+    def as_column(values, first):
+        row = lax.broadcasted_iota(jnp.int32, (QROWS, 128), 0)
+        lane = lax.broadcasted_iota(jnp.int32, (QROWS, 128), 1)
+        return jnp.sum(jnp.where(lane == row + first, values, 0.0), axis=1, keepdims=True)
+
     def attend(b, g, keys, flipped):
+        b0, half = GROUPS[g][0], STAT_ROWS[g] // 2
+
         def part(n, carry):
             q = q_all[pl.ds(2 * n, 2), :, b, :, 0:LAT].reshape(2 * SIDE * QROWS, LAT)
             k = keys()
@@ -218,28 +263,38 @@
                 e.astype(BF), v, (((1,), (1 - key_dim,)), ((), ())), preferred_element_type=F32
             )
             numer[pl.ds(2 * n, 2), :, b] = o.astype(BF).reshape(2, SIDE, QROWS, KV)
-            lane = lax.broadcasted_iota(jnp.int32, (2 * SIDE * QROWS, 128), 1)
-            shape = (2, SIDE, QROWS, 128)
-            here = (lane == b - GROUPS[g][0])
-            old_top = stats[g, 0, pl.ds(2 * n, 2)].reshape(2 * SIDE * QROWS, 128)
-            old_sum = stats[g, 1, pl.ds(2 * n, 2)].reshape(2 * SIDE * QROWS, 128)
-            stats[g, 0, pl.ds(2 * n, 2)] = jnp.where(here, top, old_top).reshape(shape)
-            stats[g, 1, pl.ds(2 * n, 2)] = jnp.where(here, total, old_sum).reshape(shape)
+            cols = pl.ds(pl.multiple_of(n * 256, 256), 256)
+            stats[g, b - b0 : b - b0 + 1, cols] = as_row(top)
+            stats[g, b - b0 + half : b - b0 + half + 1, cols] = as_row(total)
             return carry
 
         lax.fori_loop(0, 2, part, 0)
 
     def index_scores(b, keys):
+        shape = (SIDE * SIDE // 2, STEPS, HEADS_DEV, 128)
+        both = q_all[:, :, b, :, KV:QW].astype(F32).reshape((SIDE * SIDE // 2, 2) + shape[1:])
+        even, odd = both[:, 0].reshape(-1, 8, 128), both[:, 1].reshape(-1, 8, 128)
+        row = lax.broadcasted_iota(jnp.int32, even.shape, 1)
+        lane = lax.broadcasted_iota(jnp.int32, even.shape, 2)
+        upper = jnp.where(lane < ROPE, pltpu.roll(even, ROPE, 2), pltpu.roll(even, 4, 1))
+        lower = jnp.where(lane < ROPE, pltpu.roll(pltpu.roll(odd, ROPE, 2), 4, 1), odd)
+        iq_buf[...] = jnp.where(row < 4, upper, lower).reshape(-1, 128).astype(BF)
+        high = lax.broadcasted_iota(jnp.int32, (QROWS, 128), 0) % 8 < 4
+        weights = []
+        for pair in range(SIDE * SIDE // 2):
+            w_even = w_all[pair // 2, 2 * (pair % 2), b : b + 1]
+            w_odd = w_all[pair // 2, 2 * (pair % 2) + 1, b : b + 1]
+            weights.append(as_column(jnp.where(high, w_even, w_odd), 0))
+        weight = jnp.concatenate(weights, axis=0)
+
         def part(n, carry):
-            block = iq_all[:, :, b].reshape(SIDE * SIDE * IROWS, 2 * IDIM)
             k = keys(n)
             logits = lax.dot_general(
-                block[:, :IDIM], k, (((1,), (1,)), ((), ())), preferred_element_type=F32
+                iq_buf[...], k, (((1,), (1,)), ((), ())), preferred_element_type=F32
             )
-            weight = block[:, IDIM : IDIM + 1].astype(F32)
             value = jnp.maximum(logits, 0.0) * weight
             cols = pl.ds(pl.multiple_of(n * 256, 256), 256)
-            out_is[b, :, cols] = jnp.sum(value.reshape(SIDE * SIDE, IROWS, 256), axis=0)
+            out_is[b, :, cols] = jnp.sum(value.reshape(SIDE * SIDE // 2, QROWS, 256), axis=0)
             return carry
 
         lax.fori_loop(0, CTX_DEV // 256, part, 0)
@@ -264,20 +319,24 @@
 
     def reduce_copies(g, phase, way):
         b0, count = GROUPS[g]
-        span = pl.ds(b0, count)
+        span, stat = pl.ds(b0, count), pl.ds(0, STAT_ROWS[g])
         axis = way if phase == 0 else 1 - way
         copies = []
         for delta in range(1, SIDE):
             other = (mine(axis) + delta) % SIDE
+            to_y = other if axis == 1 else y
+            tile = pl.ds(pl.multiple_of(to_y * 128, 128), 128)
             if phase == 0:
-                if way == 0:
-                    src, src_st = numer.at[:, other, span, :, lanes(way)], stats.at[g, :, :, other]
-                else:
-                    src, src_st = numer.at[other, :, span, :, lanes(way)], stats.at[g, :, other]
-                dst, dst_st = ra.at[way, delta - 1, :, span], rsa.at[g, way, delta - 1]
+                src = numer.at[:, other, span, :, lanes(way)]
+                src_st, dst_st = stats.at[g, stat], rsa.at[g, way, delta - 1, stat]
+                if way == 1:
+                    src = numer.at[other, :, span, :, lanes(way)]
+                    src_st = stats.at[g, stat, tile]
+                    dst_st = rsa.at[g, way, delta - 1, stat, pl.ds(0, 128)]
+                dst = ra.at[way, delta - 1, :, span]
             else:
-                src, src_st = nb_buf.at[way, other, span], stb.at[g, way, other]
-                dst, dst_st = rb.at[way, delta - 1, span], rsb.at[g, way, delta - 1]
+                src, src_st = nb_buf.at[way, other, span], stb.at[g, way, stat, tile]
+                dst, dst_st = rb.at[way, delta - 1, span], rsb.at[g, way, delta - 1, stat]
             target = along(axis, delta)
             for which, (s, d) in enumerate(((src, dst), (src_st, dst_st))):
                 at = (g, phase, way, which, delta - 1)
@@ -288,39 +347,49 @@
         for copy in reduce_copies(g, phase, way):
             copy.start()
 
-    def merged(tops, sums):
+    def merged(g, blocks):
+        half = STAT_ROWS[g] // 2
+        tops = [block[:half] for block in blocks]
         top = tops[0]
         for value in tops[1:]:
             top = jnp.maximum(top, value)
         factors = [jnp.exp(value - top) for value in tops]
-        total = factors[0] * sums[0]
-        for factor, value in zip(factors[1:], sums[1:]):
-            total = total + factor * value
+        total = factors[0] * blocks[0][half:]
+        for factor, block in zip(factors[1:], blocks[1:]):
+            total = total + factor * block[half:]
         return top, factors, total
 
     def combine_a(g, way):
         b0, count = GROUPS[g]
+        half = STAT_ROWS[g] // 2
+        stat = slice(0, STAT_ROWS[g])
         for copy in reduce_copies(g, 0, way):
             copy.wait_recv()
+        if way == 0:
+            blocks = [stats[g, stat]] + [rsa[g, way, d, stat] for d in range(SIDE - 1)]
+            cols = slice(0, SIDE * 128)
+        else:
+            blocks = [stats[g, stat, pl.ds(pl.multiple_of(y * 128, 128), 128)]]
+            blocks += [rsa[g, way, d, stat, 0:128] for d in range(SIDE - 1)]
+            cols = pl.ds(pl.multiple_of(y * 128, 128), 128)
+        top, factors, total = merged(g, blocks)
+        stb[g, way, 0:half, cols] = top
+        stb[g, way, half : 2 * half, cols] = total
+        for d in range(SIDE):
+            fbuf[d, 0:half, cols] = factors[d]
 
         def block(j, carry):
-            if way == 0:
-                own = (stats[g, 0, j, x], stats[g, 1, j, x])
-            else:
-                own = (stats[g, 0, y, j], stats[g, 1, y, j])
-            tops = [own[0]] + [rsa[g, way, d, 0, j] for d in range(SIDE - 1)]
-            sums = [own[1]] + [rsa[g, way, d, 1, j] for d in range(SIDE - 1)]
-            top, factors, total = merged(tops, sums)
-            stb[g, way, j, 0] = top
-            stb[g, way, j, 1] = total
+            tile = pl.ds(pl.multiple_of((j if way == 0 else y) * 128, 128), 128)
+            first = (x if way == 0 else j) * QROWS
             for n in range(count):
                 if way == 0:
-                    first = numer[j, x, b0 + n, :, 0:256]
+                    own = numer[j, x, b0 + n, :, 0:256]
                 else:
-                    first = numer[y, j, b0 + n, :, 256:512]
-                acc = first.astype(F32) * factors[0][:, n : n + 1]
+                    own = numer[y, j, b0 + n, :, 256:512]
+                acc = own.astype(F32) * as_column(fbuf[0, n : n + 1, tile], first)
                 for d in range(SIDE - 1):
-                    acc = acc + ra[way, d, j, b0 + n].astype(F32) * factors[d + 1][:, n : n + 1]
+                    factor = as_column(fbuf[d + 1, n : n + 1, tile], first)
+                    acc = acc + ra[way, d, j, b0 + n].astype(F32) * factor
                 nb_buf[way, j, b0 + n] = acc.astype(BF)
             return carry
 
@@ -329,26 +398,27 @@
 
     def combine_b(g, way):
         b0, count = GROUPS[g]
+        stat = slice(0, STAT_ROWS[g])
         for copy in reduce_copies(g, 1, way):
             copy.wait_recv()
         here = mine(1 - way)
-        tops = [stb[g, way, here, 0]] + [rsb[g, way, d, 0] for d in range(SIDE - 1)]
-        sums = [stb[g, way, here, 1]] + [rsb[g, way, d, 1] for d in range(SIDE - 1)]
-        top, factors, total = merged(tops, sums)
+        blocks = [stb[g, way, stat, pl.ds(pl.multiple_of(y * 128, 128), 128)]]
+        blocks += [rsb[g, way, d, stat] for d in range(SIDE - 1)]
+        _, factors, total = merged(g, blocks)
+        factors = [factor / total for factor in factors]
         for n in range(count):
-            acc = nb_buf[way, here, b0 + n].astype(F32) * factors[0][:, n : n + 1]
+            acc = nb_buf[way, here, b0 + n].astype(F32) * as_column(factors[0][n : n + 1], x * QROWS)
             for d in range(SIDE - 1):
-                acc = acc + rb[way, d, b0 + n].astype(F32) * factors[d + 1][:, n : n + 1]
-            out_latent[b0 + n, :, way * 256 : (way + 1) * 256] = (
-                acc / total[:, n : n + 1]
-            ).astype(BF)
+                factor = as_column(factors[d + 1][n : n + 1], x * QROWS)
+                acc = acc + rb[way, d, b0 + n].astype(F32) * factor
+            out_latent[b0 + n, :, way * 256 : (way + 1) * 256] = acc.astype(BF)
 
     own_q.start()
-    own_iq.start()
+    own_w.start()
     for i in range(2):
         own_copy_a(i).start()
         start_a(i)
-    for copy in gather_copies(0):
+    for copy in gather_near(0) + weight_copies(0):
         copy.start()
     for i in range(2, 5):
         own_copy_a(i).start()
@@ -361,12 +431,16 @@
     a_to_b(1)
     b_to_z(0)
     own_q.wait()
-    own_iq.wait()
-    for copy in gather_copies(0):
+    own_w.wait()
+    for copy in gather_near(0) + weight_copies(0):
         copy.wait_recv()
-    for copy in gather_copies(1):
+    for copy in gather_far(0) + weight_copies(1):
         copy.start()
     b_to_z(1)
+    for copy in gather_far(0):
+        copy.wait_recv()
+    for copy in gather_near(1):
+        copy.start()
     a_to_b(2)
 
     for i in range(N_CH):
@@ -381,8 +455,13 @@
         finalize(i)
         if i == 1:
             out_copies("idx").start()
+        if i == 1:
+            for copy in gather_near(1):
+                copy.wait_recv()
+            for copy in gather_far(1):
+                copy.start()
         if i == 3:
-            for copy in gather_copies(1):
+            for copy in gather_far(1) + weight_copies(1):
                 copy.wait_recv()
             attend_res(0)
         elif i == 4:
@@ -434,7 +513,7 @@
         for delta in range(1, N_REQ):
             copy_z(i, delta).wait_send()
     for phase in range(2):
-        for copy in gather_copies(phase):
+        for copy in gather_near(phase) + gather_far(phase) + weight_copies(phase):
             copy.wait_send()
         for g in range(len(GROUPS)):
             for way in range(2):
@@ -456,7 +535,7 @@
         out_shape=(
             jax.ShapeDtypeStruct((NEW, PG_LOC, PAGE, LAT), BF),
             jax.ShapeDtypeStruct((NEW, PG_LOC, PAGE, IDIM), BF),
-            jax.ShapeDtypeStruct((BATCH, IROWS, CTX_DEV), F32),
+            jax.ShapeDtypeStruct((BATCH, QROWS, CTX_DEV), F32),
             jax.ShapeDtypeStruct((BATCH, QROWS, KV), BF),
             jax.ShapeDtypeStruct((N_CH, SIDE, NEW, SIDE, HALF, 128), BF),
         ),
@@ -467,23 +546,25 @@
             pltpu.VMEM((RING, N_REQ - 1) + tile, BF),
             (pltpu.VMEM((N_REQ,) + tile, BF),) * N_CH,
             pltpu.VMEM((SIDE, SIDE, BATCH, QROWS, QW), BF),
-            pltpu.VMEM((SIDE, SIDE, BATCH, IROWS, 2 * IDIM), BF),
+            pltpu.VMEM((SIDE, SIDE, 16, 128), F32),
+            pltpu.VMEM((SIDE * SIDE // 2 * QROWS, IDIM), BF),
             pltpu.VMEM((2, LAT, CTX_DEV), BF),
             pltpu.VMEM((RES, CTX_DEV, IDIM), BF),
             pltpu.VMEM((NEW, PG_LOC, PAGE, LAT), BF),
             pltpu.VMEM((NEW, PG_LOC, PAGE, IDIM), BF),
             pltpu.VMEM((SIDE, SIDE, BATCH, QROWS, KV), BF),
-            pltpu.VMEM((n_groups, 2, SIDE, SIDE, QROWS, 128), F32),
+            pltpu.VMEM((n_groups, 16, SIDE * 128), F32),
             pltpu.VMEM((2, SIDE - 1, SIDE, BATCH, QROWS, 256), BF),
-            pltpu.VMEM((n_groups, 2, SIDE - 1, 2, SIDE, QROWS, 128), F32),
+            pltpu.VMEM((n_groups, 2, SIDE - 1, 16, SIDE * 128), F32),
             pltpu.VMEM((2, SIDE, BATCH, QROWS, 256), BF),
-            pltpu.VMEM((n_groups, 2, SIDE, 2, QROWS, 128), F32),
+            pltpu.VMEM((n_groups, 2, 16, SIDE * 128), F32),
             pltpu.VMEM((2, SIDE - 1, BATCH, QROWS, 256), BF),
-            pltpu.VMEM((n_groups, 2, SIDE - 1, 2, QROWS, 128), F32),
+            pltpu.VMEM((n_groups, 2, SIDE - 1, 16, 128), F32),
+            pltpu.VMEM((SIDE, 8, SIDE * 128), F32),
             dma((N_CH, 3)), dma((N_CH, 3)), dma((N_CH, 3)), dma((N_CH, 3)),
             dma((N_CH, N_REQ - 1)), dma((N_CH, N_REQ - 1)),
             dma((N_CH,)), dma((N_CH,)), dma((3,)), dma((2,)), dma((RES,)),
-            dma((2, 2, 2, 3)), dma((2, 2, 2, 3)),
+            dma((2, 2, 2, 2)), dma((2, 2, 2, 2)), dma((2, 3)), dma((2, 3)),
             dma((n_groups, 2, 2, 2, 3)), dma((n_groups, 2, 2, 2, 3)),
         ],
         compiler_params=pltpu.CompilerParams(
@@ -511,12 +592,12 @@
     rope = jnp.concatenate([paged[..., :HALF, KV:], paged[..., HALF:, KV:]], axis=-1)
 
     absorbed = jnp.einsum("sbhn,hnc->sbhc", q_nope, w_uk, preferred_element_type=F32).astype(BF)
-    pad = jnp.zeros(q_rope.shape[:-1] + (QW - LAT,), BF)
-    queries = jnp.concatenate([absorbed, q_rope, pad], axis=-1)
+    halves = jnp.concatenate([idx_query[..., : IDIM // 2], idx_query[..., IDIM // 2 :]], axis=2)
+    queries = jnp.concatenate([absorbed, q_rope, halves], axis=-1)
     queries = queries.transpose(1, 0, 2, 3).reshape(BATCH, QROWS, QW)
-    spread = jnp.broadcast_to(idx_weight[..., None], idx_query.shape)
-    idx_queries = jnp.concatenate([idx_query, spread], axis=-1)
-    idx_queries = idx_queries.transpose(1, 0, 2, 3).reshape(BATCH, IROWS, 2 * IDIM)
+    weights = jnp.concatenate([idx_weight, idx_weight], axis=2).astype(F32)
+    weights = weights.transpose(1, 0, 2).reshape(BATCH, QROWS)
+    weights = jnp.pad(weights, ((0, 16 - BATCH), (0, 128 - QROWS)))
 
     here = (selected % (SIDE * SIDE) == pos_index)[..., None]
     slots = jnp.arange(PG_LOC, dtype=jnp.int32)
@@ -529,10 +610,10 @@
     new_latent, new_index, raw, latent, _ = run_kernel(
         chosen.astype(jnp.int32), sources.astype(jnp.int32), new_lengths,
         paged, arrive_index.reshape(NEW, SIDE, SIDE, PAGE, IDIM), rope,
-        queries, idx_queries, res_latent[:, 0].transpose(0, 2, 1), res_index[:, 0], bias,
+        queries, weights, res_latent[:, 0].transpose(0, 2, 1), res_index[:, 0], bias,
     )
 
-    scored = jnp.sum(raw.reshape(BATCH, STEPS, IHEADS_DEV, CTX_DEV), axis=2) * IDIM ** (-0.5)
+    scored = jnp.sum(raw.reshape(BATCH, STEPS, HEADS_DEV, CTX_DEV), axis=2) * IDIM ** (-0.5)
     lengths = jnp.concatenate([res_len, new_lengths])
     offsets = jnp.arange(CTX_DEV, dtype=jnp.int32)
     logical = (offsets // PAGE * (SIDE * SIDE) + pos_index) * PAGE + offsets % PAGE

time: 271 us -> 232 us (0.86)
  Pallas kernels: 236 us -> 198 us
    pallas_call x1, Pallas kernels: 236 us -> 198 us  [run_kernel(): pl.pallas_call(kernel, out_shape=(jax.ShapeDtypeStruct((NEW, PG_LOC, PAGE...]
    unnamed x31 -> x32, local copies, waits for them, and re-layouts: 18.2 us -> 18.6 us
where the time goes in v2:
time: 232 us; the launch traced here: 230 us
  Pallas kernels  198 us (85%)
  local copies, waits for them, and re-layouts  25.3 us (11%)
  other arithmetic  5.26 us (2%)
    pallas_call x1, Pallas kernels, run_kernel(): pl.pallas_call(kernel, out_shape=(jax.ShapeDtypeStruct((NEW, PG_LOC, PAGE...  198 us
    unnamed x32, local copies, waits for them, and re-layouts  18.6 us

profile of v2, /device:TPU:0, one launch (start us, length us, event | category | flops | bytes accessed | tf_op | source)
XLA Modules:
  0.0 230.3 jit_solution(16023436667785493642)
XLA Ops:
  0.6 0.0 copy-start
  0.7 0.8 reshape.142
  1.4 0.6 select_reduce_fusion
  2.1 0.0 copy-start.8
  2.1 1.9 gather_fusion
  3.9 7.7 %copy.45 = bf16[4,1024,576]{2,1,0:T(8,128)(2,1)} copy(bf16[4,1024,576]{1,2,0:T(8,128)(2,1)} %param.17) | data formatting | bytes 9437184 | tf_op args[3]
  11.6 0.0 copy-done.8
  11.6 1.3 fusion.22
  12.9 0.0 copy-start.4
  12.9 0.0 copy-start.10
  13.0 1.1 pad_maximum_fusion.rope
  14.1 0.0 copy-done.4
  14.1 0.0 copy-start.5
  14.1 0.1 fusion.23
  14.2 0.0 copy-done
  14.2 0.0 copy-done.10
  14.2 0.3 fusion
  14.5 0.5 copy-done.5
  15.0 0.0 copy-start.6
  15.0 0.1 maximum_bitcast_fusion
  15.1 1.0 copy.70
  16.1 0.0 copy-start.7
  16.1 0.0 copy-done.6
  16.2 0.8 fusion.6
  17.0 0.1 broadcast_in_dim.65
  17.2 0.2 select_n.76
  17.4 1.2 broadcast_bitcast_fusion.bias
  18.6 0.0 copy-done.7
  18.6 0.1 copy.62
  18.7 0.6 pad_convert_fusion.wown
  19.3 198.2 %decode_step.1 = (bf16[4,16,64,576]{3,2,1,0:T(8,128)(2,1)}, bf16[4,16,64,128]{3,2,1,0:T(8,128)(2,1)}, f32[10,32,1024]{2,1,0:T(8,128)}, bf16[10,32,512]{2,1,0:T(8,128)(2,1)}, bf16[11,4,4,4,32,128]{5,4,3,2,1,0:T(8,128)(2,1)}) custom-call(s32[8]{0:T(128)} %get-tuple-element.29.chosen, s32[4]{0:T(128)} %copy-done.8, s32[4]{0:T(128)} %gather_fusion, ...), custom_call_target="tpu_custom_call" | custom-call | tf_op jit(solution)/shard_map/decode_step/pallas_call | solution.py:533
  217.6 0.0 copy-start.9
  217.6 0.0 copy-start.11
  217.6 1.7 bitcast_reduce_fusion
  219.3 0.0 copy-done.9
  219.3 0.0 copy-done.11
  219.3 0.1 pad_add_fusion
  219.4 0.1 broadcast_compare_fusion
  219.4 0.1 select_bitcast_fusion
  219.5 0.8 copy.58
  220.4 0.0 copy-start.2
  220.4 7.7 %copy.56 = bf16[4,1,1024,576]{2,3,1,0:T(8,128)(2,1)} copy(bf16[4,1,1024,576]{3,2,0,1:T(8,128)(2,1)} %bitcast.58) | data formatting | bytes 9437184
  228.1 0.0 copy-done.2
  228.1 0.0 copy-done.3
  228.1 0.4 fusion.1
  228.5 0.7 copy.59
  229.2 0.1 copy-done.1
  229.3 1.0 copy.72
  (16 shorter events, 0.2 us)
Async XLA Ops:
  0.6 13.6 %copy-start = (bf16[4,10,8,128]{3,2,1,0:T(8,128)(2,1)S(1)}, bf16[4,10,8,128]{3,2,1,0:T(8,128)(2,1)}, u32[]{:S(2)}) copy-start(bf16[4,10,8,128]{3,2,1,0:T(8,128)(2,1)} %param.21) | copy-start | bytes 245764
  2.1 9.5 %copy-start.8 = (s32[4]{0:T(128)}, s32[4]{0:T(128)S(1)}, u32[]{:S(2)}) copy-start(s32[4]{0:T(128)S(1)} %get-tuple-element.28.sources) | copy-start | bytes 52
  12.9 1.1 copy-start.4
  12.9 1.3 copy-start.10
  14.1 0.9 copy-start.5
  15.0 1.2 copy-start.6
  16.1 2.4 %copy-start.7 = (bf16[4,10,4]{1,2,0:T(4,128)(2,1)S(1)}, bf16[4,10,4]{1,2,0:T(4,128)(2,1)}, u32[]{:S(2)}) copy-start(bf16[4,10,4]{1,2,0:T(4,128)(2,1)} %param.26) | copy-start | bytes 964
  217.6 1.7 copy-start.9
  217.6 1.7 copy-start.11
  220.4 7.7 %copy-start.2 = (bf16[8,512,128]{2,1,0:T(8,128)(2,1)S(1)}, bf16[8,512,128]{2,1,0:T(8,128)(2,1)}, u32[]{:S(2)}) copy-start(bf16[8,512,128]{2,1,0:T(8,128)(2,1)} %param.24) | copy-start | bytes 3145732
  220.4 7.7 %copy-start.3 = (bf16[10,32,512]{2,1,0:T(8,128)(2,1)S(1)}, bf16[10,32,512]{2,1,0:T(8,128)(2,1)}, u32[]{:S(2)}) copy-start(bf16[10,32,512]{2,1,0:T(8,128)(2,1)} %get-tuple-element.11) | copy-start | bytes 983044
  228.1 1.2 copy-start.1

commit v3 on v2

--- a/solution.py
+++ b/solution.py
@@ -16,22 +16,20 @@
 MESH = pl.DeviceIdType.MESH
 SCALE = (NOPE + ROPE) ** (-0.5)
 
-CHUNKS = (
-    [("idx", 0, 0), ("idx", 0, 1), ("rope", 0, 0)]
-    + [("lat", j, h) for j in range(KV // 128) for h in range(2)]
-)
-N_CH = len(CHUNKS)
+N_IDX, N_LAT, DEPTH = 2, LAT // 64, 64
+N_CH = N_IDX + N_LAT
+N_XF = (N_LAT + 1) // 2
 RING = 3
-GROUPS = ((0, 6), (6, 2), (8, 2))
-STAT_ROWS = (16, 8, 8)
+GROUPS = ((0, 6), (6, 1), (7, 1), (8, 1), (9, 1))
+STAT_ROWS = (16, 8, 8, 8, 8)
 
 
 def kernel(
-    chosen, sources, limits, lat, idx, rope, qown, wown, reslat, residx, bias,
-    out_lat, out_idx, out_is, out_latent, a_buf,
-    b_bufs, zsend, zrecvs, q_all, w_all, iq_buf, kbuf, ki_res, kfin, kifin, numer, stats,
+    chosen, sources, limits, lat, idx, qown, wown, reslat, residx, bias,
+    out_lat, out_idx, out_is, out_latent, a_idx, a_lat,
+    ay_bufs, b_idx, b_lat, loads, pack_x, pack_y, unpacked, zs_idx, zs_lat, zrecvs, q_all, w_all, iq_buf, kbuf, ki_res, kfin, kifin, numer, stats,
     ra, rsa, nb_buf, stb, rb, rsb, fbuf,
-    sa_s, sa_r, sb_s, sb_r, sz_s, sz_r, own_a, own_b, load_sem, out_sem, kb_sem,
+    sa_s, sa_r, sb_s, sb_r, sz_s, sz_r, own_a, own_b, lat_sem, load_sem, out_sem, kb_sem,
     ag_s, ag_r, aw_s, aw_r, rs_s, rs_r,
 ):
     req = lax.axis_index("req")
@@ -63,23 +61,39 @@
     def first_axis(i):
         return i % 2
 
-    def chunk_source(i, coord):
-        kind, plane, half = CHUNKS[i]
-        if kind == "rope":
-            ref, rows, lanes = rope, pl.ds(0, HALF), pl.ds(0, 128)
-        elif kind == "idx":
-            ref, rows, lanes = idx, pl.ds(half * HALF, HALF), pl.ds(0, 128)
-        else:
-            ref, rows, lanes = lat, pl.ds(half * HALF, HALF), pl.ds(plane * 128, 128)
+    def depth(i):
+        return pl.ds((i - N_IDX) * DEPTH, DEPTH)
+
+    def load_lat(i):
+        n = (i - N_IDX) // 2
+        return pltpu.make_async_copy(lat.at[:, depth(i)], loads.at[n % 2], lat_sem.at[n])
+
+    def a_slot(i):
+        if i < N_IDX:
+            return a_idx.at[i]
+        return a_lat.at[(i - N_IDX) // 2] if first_axis(i) == 0 else ay_bufs[(i - N_IDX) // 2]
+
+    def a_source(i, coord):
+        if i < N_IDX:
+            rows = pl.ds(i * HALF, HALF)
+            return idx.at[:, :, coord, rows] if first_axis(i) == 0 else idx.at[:, coord, :, rows]
         if first_axis(i) == 0:
-            return ref.at[:, :, coord, rows, lanes]
-        return ref.at[:, coord, :, rows, lanes]
+            return pack_x.at[(i - N_IDX) // 2 % 2, coord]
+        return lat.at[:, depth(i), pl.ds(pl.multiple_of(coord * 256, 256), 256)]
+
+    def b_slot(i):
+        return b_idx[i] if i < N_IDX else b_lat[i - N_IDX]
+
+    def b_source(i, coord):
+        if i >= N_IDX and first_axis(i) == 1:
+            return pack_y.at[(i - N_IDX) // 2 % 2, coord]
+        return a_slot(i).at[:, :, coord]
 
     def copies_a(i):
         axis = first_axis(i)
         return [
             remote(
-                chunk_source(i, (mine(axis) + delta) % SIDE), a_buf.at[i, mine(axis)],
+                a_source(i, (mine(axis) + delta) % SIDE), a_slot(i).at[mine(axis)],
                 sa_s.at[i, delta - 1], sa_r.at[i, delta - 1], along(axis, delta),
             )
             for delta in range(1, SIDE)
@@ -87,13 +101,13 @@
 
     def own_copy_a(i):
         coord = mine(first_axis(i))
-        return pltpu.make_async_copy(chunk_source(i, coord), a_buf.at[i, coord], own_a.at[i])
+        return pltpu.make_async_copy(a_source(i, coord), a_slot(i).at[coord], own_a.at[i])
 
     def copies_b(i):
         axis = 1 - first_axis(i)
         return [
             remote(
-                a_buf.at[i, :, :, (mine(axis) + delta) % SIDE], b_bufs[i].at[mine(axis)],
+                b_source(i, (mine(axis) + delta) % SIDE), b_slot(i).at[mine(axis)],
                 sb_s.at[i, delta - 1], sb_r.at[i, delta - 1], along(axis, delta),
             )
             for delta in range(1, SIDE)
@@ -101,15 +115,62 @@
 
     def own_copy_b(i):
         coord = mine(1 - first_axis(i))
-        return pltpu.make_async_copy(a_buf.at[i, :, :, coord], b_bufs[i].at[coord], own_b.at[i])
+        return pltpu.make_async_copy(b_source(i, coord), b_slot(i).at[coord], own_b.at[i])
+
+    def z_send(i):
+        return zs_idx.at[i] if i < N_IDX else zs_lat.at[(i - N_IDX) % RING]
 
     def copy_z(i, delta):
         return remote(
-            zsend.at[i % RING, delta - 1], zrecvs[i].at[req],
+            z_send(i).at[delta - 1], zrecvs[i].at[req],
             sz_s.at[i, delta - 1], sz_r.at[i, delta - 1], ((req + delta) % N_REQ, pos),
         )
 
+    sent = set()
+
+    def drain(kind, i):
+        if (kind, i) in sent:
+            return
+        sent.add((kind, i))
+        copies = {"a": copies_a, "b": copies_b}.get(kind)
+        if copies is None:
+            copies = lambda n: [copy_z(n, delta) for delta in range(1, N_REQ)]
+        for copy in copies(i):
+            copy.wait_send()
+
+    low = lax.broadcasted_iota(jnp.int32, (DEPTH, 128), 1) < PAGE
+
+    def swapped(first, second):
+        first, second = first.astype(F32), second.astype(F32)
+        lows = jnp.where(low, first, pltpu.roll(second, PAGE, 1))
+        highs = jnp.where(low, pltpu.roll(first, PAGE, 1), second)
+        return lows.astype(BF), highs.astype(BF)
+
+    def lane_tile(n):
+        return pl.ds(pl.multiple_of(n * 128, 128), 128)
+
     def start_a(i):
+        if i >= N_IDX and first_axis(i) == 0:
+            n = (i - N_IDX) // 2
+            load_lat(i).wait()
+            if n >= 2:
+                drain("a", i - 4)
+
+            def pack(row, carry):
+                for pair in range(2):
+                    for kp in range(2):
+                        tile = lane_tile(row * 2 + pair)
+                        lows, highs = swapped(
+                            loads[n % 2, 2 * kp, :, tile], loads[n % 2, 2 * kp + 1, :, tile]
+                        )
+                        pack_x[n % 2, 2 * pair, kp, row] = lows
+                        pack_x[n % 2, 2 * pair + 1, kp, row] = highs
+                return carry
+
+            lax.fori_loop(0, SIDE, pack, 0)
+            if i + 4 < N_CH:
+                load_lat(i + 4).start()
+        own_copy_a(i).start()
         for copy in copies_a(i):
             copy.start()
 
@@ -117,6 +178,23 @@
         own_copy_a(i).wait()
         for copy in copies_a(i):
             copy.wait_recv()
+        if i >= N_IDX and first_axis(i) == 1:
+            n = (i - N_IDX) // 2
+            if n >= 2:
+                drain("b", i - 4)
+
+            def pack(row, carry):
+                for pair in range(2):
+                    tile = slice(pair * 128, (pair + 1) * 128)
+                    for kp in range(2):
+                        lows, highs = swapped(
+                            ay_bufs[n][row, 2 * kp, :, tile], ay_bufs[n][row, 2 * kp + 1, :, tile]
+                        )
+                        pack_y[n % 2, 2 * pair, row, kp] = lows
+                        pack_y[n % 2, 2 * pair + 1, row, kp] = highs
+                return carry
+
+            lax.fori_loop(0, SIDE, pack, 0)
         for copy in copies_b(i):
             copy.start()
         own_copy_b(i).start()
@@ -125,18 +203,34 @@
         own_copy_b(i).wait()
         for copy in copies_b(i):
             copy.wait_recv()
-        if i >= RING:
-            for delta in range(1, N_REQ):
-                copy_z(i - RING, delta).wait_send()
+        if i >= N_IDX + RING:
+            drain("z", i - RING)
+        buf = b_slot(i)
+        if i >= N_IDX:
+            def unpack(row, carry):
+                for pair in range(2):
+                    for kp in range(2):
+                        if first_axis(i) == 0:
+                            even, odd = buf[row, 2 * pair, kp], buf[row, 2 * pair + 1, kp]
+                        else:
+                            even, odd = buf[2 * pair, row, kp], buf[2 * pair + 1, row, kp]
+                        lows, highs = swapped(even, odd)
+                        unpacked[2 * kp, :, lane_tile(row * 2 + pair)] = lows
+                        unpacked[2 * kp + 1, :, lane_tile(row * 2 + pair)] = highs
+                return carry
+
+            lax.fori_loop(0, SIDE, unpack, 0)
+
+        def block(k):
+            return buf[:, :, k] if i < N_IDX else unpacked[k]
 
         def stage(delta, carry):
-            k = chosen[(req + delta) % N_REQ]
-            zsend[i % RING, delta - 1] = b_bufs[i][:, :, k]
+            z_send(i)[delta - 1] = block(chosen[(req + delta) % N_REQ])
             copy_z(i, delta).start()
             return carry
 
         lax.fori_loop(1, N_REQ, stage, 0)
-        zrecvs[i][req] = b_bufs[i][:, :, chosen[req]]
+        zrecvs[i][req] = block(chosen[req])
 
     def wait_z(i):
         for delta in range(1, N_REQ):
@@ -147,35 +241,34 @@
             return pltpu.make_async_copy(kifin, out_idx, out_sem.at[0])
         return pltpu.make_async_copy(kfin, out_lat, out_sem.at[1])
 
-    def finalize(i):
-        kind, plane, half = CHUNKS[i]
-        by_x = first_axis(i) == 0
-
+    def finalize_idx(i):
         def page(n, carry):
             outer, inner = n // SIDE, n % SIDE
-            l = outer * SIDE + inner if by_x else inner * SIDE + outer
-            base = (l * (SIDE * SIDE) + pos) * PAGE
+            l = outer * SIDE + inner if first_axis(i) == 0 else inner * SIDE + outer
+            base = (l * (SIDE * SIDE) + pos) * PAGE + i * HALF
             row = lax.broadcasted_iota(jnp.int32, (HALF, 128), 0)
             for k in range(NEW):
-                tile = zrecvs[i][sources[k], outer, inner]
-                if kind == "rope":
-                    for part in range(2):
-                        keep = row[:, :ROPE] + (base + part * HALF) < limits[k]
-                        value = tile[:, part * ROPE : (part + 1) * ROPE].astype(F32)
-                        kfin[k, l, part * HALF : (part + 1) * HALF, KV:LAT] = jnp.where(
-                            keep, value, 0.0
-                        ).astype(BF)
-                else:
-                    keep = row + (base + half * HALF) < limits[k]
-                    value = jnp.where(keep, tile.astype(F32), 0.0).astype(BF)
-                    rows = slice(half * HALF, (half + 1) * HALF)
-                    if kind == "idx":
-                        kifin[k, l, rows, :] = value
-                    else:
-                        kfin[k, l, rows, plane * 128 : (plane + 1) * 128] = value
+                tile = zrecvs[i][sources[k], outer, inner].astype(F32)
+                value = jnp.where(row + base < limits[k], tile, 0.0).astype(BF)
+                kifin[k, l, i * HALF : (i + 1) * HALF, :] = value
             return carry
 
         lax.fori_loop(0, SIDE * SIDE, page, 0)
+
+    def finalize(i):
+        if i < N_IDX:
+            return finalize_idx(i)
+
+        def tiles(n, carry):
+            lane = lax.broadcasted_iota(jnp.int32, (DEPTH, 128), 1)
+            logical = (2 * n + lane // PAGE) * (SIDE * SIDE * PAGE) + pos * PAGE + lane % PAGE
+            for k in range(NEW):
+                tile = zrecvs[i][sources[k], :, lane_tile(n)].astype(F32)
+                value = jnp.where(logical < limits[k], tile, 0.0).astype(BF)
+                kfin[k, depth(i), lane_tile(n)] = value
+            return carry
+
+        lax.fori_loop(0, CTX_DEV // 128, tiles, 0)
 
     spans = (pl.ds(0, BATCH // 2), pl.ds(BATCH // 2, BATCH // 2))
 
@@ -245,22 +338,20 @@
         lane = lax.broadcasted_iota(jnp.int32, (QROWS, 128), 1)
         return jnp.sum(jnp.where(lane == row + first, values, 0.0), axis=1, keepdims=True)
 
-    def attend(b, g, keys, flipped):
+    def attend(b, g, keys):
         b0, half = GROUPS[g][0], STAT_ROWS[g] // 2
 
         def part(n, carry):
             q = q_all[pl.ds(2 * n, 2), :, b, :, 0:LAT].reshape(2 * SIDE * QROWS, LAT)
             k = keys()
-            key_dim = 0 if flipped else 1
-            s = lax.dot_general(q, k, (((1,), (key_dim,)), ((), ())), preferred_element_type=F32)
+            s = jnp.dot(q, k, preferred_element_type=F32)
             s = (s * SCALE).reshape(2 * SIDE, QROWS, CTX_DEV) + bias[b][None]
             s = s.reshape(2 * SIDE * QROWS, CTX_DEV)
             top = jnp.maximum(jnp.max(s, axis=1, keepdims=True), -1e29)
             e = jnp.exp(s - top)
             total = jnp.sum(e, axis=1, keepdims=True)
-            v = k[:KV] if flipped else k[:, :KV]
             o = lax.dot_general(
-                e.astype(BF), v, (((1,), (1 - key_dim,)), ((), ())), preferred_element_type=F32
+                e.astype(BF), k[:KV], (((1,), (1,)), ((), ())), preferred_element_type=F32
             )
             numer[pl.ds(2 * n, 2), :, b] = o.astype(BF).reshape(2, SIDE, QROWS, KV)
             cols = pl.ds(pl.multiple_of(n * 256, 256), 256)
@@ -301,12 +392,12 @@
 
     def attend_res(b):
         load_k(b).wait()
-        attend(b, 0, lambda: kbuf[b % 2], True)
+        attend(b, 0, lambda: kbuf[b % 2])
         if b + 2 < RES:
             load_k(b + 2).start()
 
     def attend_new(k, g):
-        attend(RES + k, g, lambda: kfin[k].reshape(CTX_DEV, LAT), False)
+        attend(RES + k, g, lambda: kfin[k])
 
     def index_res(b):
         index_scores(b, lambda n: ki_res[b, pl.ds(pl.multiple_of(n * 256, 256), 256)])
@@ -413,105 +504,110 @@
                 acc = acc + rb[way, d, b0 + n].astype(F32) * factor
             out_latent[b0 + n, :, way * 256 : (way + 1) * 256] = acc.astype(BF)
 
+    def start(copies):
+        for copy in copies:
+            copy.start()
+
+    def arrived(copies):
+        for copy in copies:
+            copy.wait_recv()
+
+    load_lat(N_IDX).start()
+    load_lat(N_IDX + 2).start()
+    start_a(0)
+    start_a(1)
     own_q.start()
     own_w.start()
-    for i in range(2):
-        own_copy_a(i).start()
-        start_a(i)
-    for copy in gather_near(0) + weight_copies(0):
-        copy.start()
-    for i in range(2, 5):
-        own_copy_a(i).start()
-        start_a(i)
     load_ki.start()
     load_k(0).start()
     load_k(1).start()
+    start_a(2)
+    start_a(3)
     stats[...] = jnp.zeros_like(stats)
     a_to_b(0)
     a_to_b(1)
+    start(gather_near(0) + weight_copies(0))
+    start_a(4)
     b_to_z(0)
+    a_to_b(2)
+    start_a(5)
+    b_to_z(1)
+    a_to_b(3)
     own_q.wait()
     own_w.wait()
-    for copy in gather_near(0) + weight_copies(0):
-        copy.wait_recv()
-    for copy in gather_far(0) + weight_copies(1):
-        copy.start()
-    b_to_z(1)
-    for copy in gather_far(0):
-        copy.wait_recv()
-    for copy in gather_near(1):
-        copy.start()
-    a_to_b(2)
+    arrived(gather_near(0) + weight_copies(0))
+    start(gather_far(0) + weight_copies(1))
+    start_a(6)
+    b_to_z(2)
+    a_to_b(4)
 
     for i in range(N_CH):
         wait_z(i)
-        if i + 2 < N_CH:
-            b_to_z(i + 2)
         if i + 3 < N_CH:
-            a_to_b(i + 3)
+            b_to_z(i + 3)
         if i + 5 < N_CH:
-            own_copy_a(i + 5).start()
-            start_a(i + 5)
+            a_to_b(i + 5)
+        if i + 7 < N_CH:
+            start_a(i + 7)
         finalize(i)
-        if i == 1:
+        if i == 0:
+            arrived(gather_far(0))
+            start(gather_near(1))
+        elif i == 1:
             out_copies("idx").start()
-        if i == 1:
-            for copy in gather_near(1):
-                copy.wait_recv()
-            for copy in gather_far(1):
-                copy.start()
-        if i == 3:
-            for copy in gather_far(1) + weight_copies(1):
-                copy.wait_recv()
+        elif i == 2:
+            arrived(gather_near(1))
+            start(gather_far(1))
+        elif i == 4:
+            arrived(gather_far(1) + weight_copies(1))
             attend_res(0)
-        elif i == 4:
             attend_res(1)
+        elif i == 5:
             attend_res(2)
             attend_res(3)
-        elif i == 5:
+            load_ki.wait()
+            index_res(0)
+        elif i == 6:
             attend_res(4)
             attend_res(5)
             for way in range(2):
                 start_reduce(0, 0, way)
-            load_ki.wait()
-            index_res(0)
             index_res(1)
-        elif i == 6:
+        elif i == 7:
             for b in range(2, RES):
                 index_res(b)
-        elif i == 7:
+        elif i == 8:
             for way in range(2):
                 combine_a(0, way)
             index_new(0)
             index_new(1)
-        elif i == 8:
+        elif i == 9:
             index_new(2)
             index_new(3)
-        elif i == 9:
+        if i == N_CH - 1:
+            out_copies("lat").start()
+            attend_new(0, 1)
+            for way in range(2):
+                start_reduce(1, 0, way)
+            attend_new(1, 2)
+            for way in range(2):
+                start_reduce(2, 0, way)
             for way in range(2):
                 combine_b(0, way)
-    out_copies("lat").start()
-    attend_new(0, 1)
-    attend_new(1, 1)
-    for way in range(2):
-        start_reduce(1, 0, way)
-    attend_new(2, 2)
-    attend_new(3, 2)
-    for way in range(2):
-        start_reduce(2, 0, way)
-    for g in (1, 2):
+    for k in (2, 3):
+        attend_new(k, k + 1)
+        for way in range(2):
+            start_reduce(k + 1, 0, way)
+    for g in (1, 2, 3, 4):
         for way in range(2):
             combine_a(g, way)
-    for g in (1, 2):
+    for g in (1, 2, 3, 4):
         for way in range(2):
             combine_b(g, way)
 
     for i in range(N_CH):
-        for copy in copies_a(i) + copies_b(i):
-            copy.wait_send()
-    for i in range(N_CH - RING, N_CH):
-        for delta in range(1, N_REQ):
-            copy_z(i, delta).wait_send()
+        for kind in ("a", "b", "z"):
+            drain(kind, i)
     for phase in range(2):
         for copy in gather_near(phase) + gather_far(phase) + weight_copies(phase):
             copy.wait_send()
@@ -533,24 +629,33 @@
     return pl.pallas_call(
         kernel,
         out_shape=(
-            jax.ShapeDtypeStruct((NEW, PG_LOC, PAGE, LAT), BF),
+            jax.ShapeDtypeStruct((NEW, LAT, CTX_DEV), BF),
             jax.ShapeDtypeStruct((NEW, PG_LOC, PAGE, IDIM), BF),
             jax.ShapeDtypeStruct((BATCH, QROWS, CTX_DEV), F32),
             jax.ShapeDtypeStruct((BATCH, QROWS, KV), BF),
-            jax.ShapeDtypeStruct((N_CH, SIDE, NEW, SIDE, HALF, 128), BF),
+            jax.ShapeDtypeStruct((N_IDX, SIDE, NEW, SIDE, HALF, 128), BF),
+            jax.ShapeDtypeStruct((N_XF, SIDE, 2, SIDE, DEPTH, 128), BF),
         ),
-        in_specs=[smem] * 3 + [hbm] * 7 + [vmem],
-        out_specs=(hbm, hbm, vmem, vmem, hbm),
+        in_specs=[smem] * 3 + [hbm] * 6 + [vmem],
+        out_specs=(hbm, hbm, vmem, vmem, hbm, hbm),
         scratch_shapes=[
-            (pltpu.VMEM((SIDE, SIDE, NEW, HALF, 128), BF),) * N_CH,
-            pltpu.VMEM((RING, N_REQ - 1) + tile, BF),
-            (pltpu.VMEM((N_REQ,) + tile, BF),) * N_CH,
+            (pltpu.VMEM((SIDE, NEW, DEPTH, 256), BF),) * (N_LAT - N_XF),
+            (pltpu.VMEM((SIDE, SIDE, NEW, HALF, 128), BF),) * N_IDX,
+            (pltpu.VMEM((SIDE, SIDE, 2, DEPTH, 128), BF),) * N_LAT,
+            pltpu.VMEM((2, NEW, DEPTH, CTX_DEV), BF),
+            pltpu.VMEM((2, SIDE, 2, SIDE, DEPTH, 128), BF),
+            pltpu.VMEM((2, SIDE, SIDE, 2, DEPTH, 128), BF),
+            pltpu.VMEM((NEW, DEPTH, CTX_DEV), BF),
+            pltpu.VMEM((N_IDX, N_REQ - 1) + tile, BF),
+            pltpu.VMEM((RING, N_REQ - 1, DEPTH, CTX_DEV), BF),
+            (pltpu.VMEM((N_REQ,) + tile, BF),) * N_IDX
+            + (pltpu.VMEM((N_REQ, DEPTH, CTX_DEV), BF),) * N_LAT,
             pltpu.VMEM((SIDE, SIDE, BATCH, QROWS, QW), BF),
             pltpu.VMEM((SIDE, SIDE, 16, 128), F32),
             pltpu.VMEM((SIDE * SIDE // 2 * QROWS, IDIM), BF),
             pltpu.VMEM((2, LAT, CTX_DEV), BF),
             pltpu.VMEM((RES, CTX_DEV, IDIM), BF),
-            pltpu.VMEM((NEW, PG_LOC, PAGE, LAT), BF),
+            pltpu.VMEM((NEW, LAT, CTX_DEV), BF),
             pltpu.VMEM((NEW, PG_LOC, PAGE, IDIM), BF),
             pltpu.VMEM((SIDE, SIDE, BATCH, QROWS, KV), BF),
             pltpu.VMEM((n_groups, 16, SIDE * 128), F32),
@@ -563,7 +668,7 @@
             pltpu.VMEM((SIDE, 8, SIDE * 128), F32),
             dma((N_CH, 3)), dma((N_CH, 3)), dma((N_CH, 3)), dma((N_CH, 3)),
             dma((N_CH, N_REQ - 1)), dma((N_CH, N_REQ - 1)),
-            dma((N_CH,)), dma((N_CH,)), dma((3,)), dma((2,)), dma((RES,)),
+            dma((N_CH,)), dma((N_CH,)), dma((N_XF,)), dma((3,)), dma((2,)), dma((RES,)),
             dma((2, 2, 2, 2)), dma((2, 2, 2, 2)), dma((2, 3)), dma((2, 3)),
             dma((n_groups, 2, 2, 2, 3)), dma((n_groups, 2, 2, 2, 3)),
         ],
@@ -588,9 +693,6 @@
     sources = jnp.sum(jnp.where(routing == req_index, group_ids[:, None], 0), axis=0)
     new_lengths = arrive_len[sources * NEW + arrival_ids]
 
-    paged = arrive_latent.reshape(NEW, SIDE, SIDE, PAGE, LAT)
-    rope = jnp.concatenate([paged[..., :HALF, KV:], paged[..., HALF:, KV:]], axis=-1)
-
     absorbed = jnp.einsum("sbhn,hnc->sbhc", q_nope, w_uk, preferred_element_type=F32).astype(BF)
     halves = jnp.concatenate([idx_query[..., : IDIM // 2], idx_query[..., IDIM // 2 :]], axis=2)
     queries = jnp.concatenate([absorbed, q_rope, halves], axis=-1)
@@ -607,9 +709,9 @@
         bias.transpose(1, 0, 2)[:, :, None, :], (BATCH, STEPS, HEADS_DEV, CTX_DEV)
     ).reshape(BATCH, QROWS, CTX_DEV)
 
-    new_latent, new_index, raw, latent, _ = run_kernel(
+    new_latent, new_index, raw, latent, _, _ = run_kernel(
         chosen.astype(jnp.int32), sources.astype(jnp.int32), new_lengths,
-        paged, arrive_index.reshape(NEW, SIDE, SIDE, PAGE, IDIM), rope,
+        arrive_latent.transpose(0, 2, 1), arrive_index.reshape(NEW, SIDE, SIDE, PAGE, IDIM),
         queries, weights, res_latent[:, 0].transpose(0, 2, 1), res_index[:, 0], bias,
     )
 
@@ -623,7 +725,7 @@
     latent = latent.reshape(BATCH, STEPS, HEADS_DEV, KV)
     head_out = jnp.einsum("bshc,hcd->sbhd", latent, w_uv, preferred_element_type=F32).astype(BF)
     return (
-        new_latent.reshape(NEW, 1, CTX_DEV, LAT),
+        new_latent.transpose(0, 2, 1).reshape(NEW, 1, CTX_DEV, LAT),
         new_index.reshape(NEW, 1, CTX_DEV, IDIM),
         index_scores,
         head_out,

time: 232 us -> 206 us (0.89)
  Pallas kernels: 198 us -> 183 us
  local copies, waits for them, and re-layouts: 25.3 us -> 13.9 us
    pallas_call x1, Pallas kernels: 198 us -> 183 us  [run_kernel(): pl.pallas_call(kernel, out_shape=(jax.ShapeDtypeStruct((NEW, LAT, CTX_DEV...]
    unnamed x32 -> x27, local copies, waits for them, and re-layouts: 18.6 us -> 7.72 us
where the time goes in v3:
time: 206 us; the launch traced here: 204 us
  Pallas kernels  183 us (89%)
  local copies, waits for them, and re-layouts  13.9 us (7%)
  other arithmetic  4.27 us (2%)
    pallas_call x1, Pallas kernels, run_kernel(): pl.pallas_call(kernel, out_shape=(jax.ShapeDtypeStruct((NEW, LAT, CTX_DEV...  183 us
    unnamed x27, local copies, waits for them, and re-layouts  7.72 us

profile of v3, /device:TPU:0, one launch (start us, length us, event | category | flops | bytes accessed | tf_op | source)
XLA Modules:
  0.0 204.4 jit_solution(3152009885351647859)
XLA Ops:
  0.6 0.0 copy-start
  0.7 0.8 reshape.139
  1.4 0.6 select_reduce_fusion
  2.1 0.0 copy-start.7
  2.1 1.8 gather_fusion
  3.9 0.0 copy-start.4
  3.9 0.9 fusion.22
  4.9 0.0 copy-done
  4.9 1.5 fusion
  6.4 0.0 copy-done.7
  6.4 0.0 copy-done.4
  6.4 0.0 copy-start.5
  6.5 0.1 maximum_bitcast_fusion
  6.6 1.0 copy.67
  7.6 0.0 copy-start.6
  7.6 0.0 copy-done.5
  7.7 0.8 fusion.6
  8.5 0.1 broadcast_in_dim.65
  8.6 0.2 select_n.76
  8.8 1.2 broadcast_bitcast_fusion.bias
  10.0 0.0 copy-done.6
  10.1 0.1 copy.59
  10.1 0.6 pad_convert_fusion.wown
  10.8 183.5 %decode_step.1 = (bf16[4,576,1024]{2,1,0:T(8,128)(2,1)}, bf16[4,16,64,128]{3,2,1,0:T(8,128)(2,1)}, f32[10,32,1024]{2,1,0:T(8,128)}, bf16[10,32,512]{2,1,0:T(8,12...) custom-call(s32[8]{0:T(128)} %get-tuple-element.27.chosen, s32[4]{0:T(128)} %copy-done.7, ...), custom_call_target="tpu_custom_call" | custom-call | tf_op jit(solution)/shard_map/decode_step/pallas_call | solution.py:629
  194.2 0.0 copy-start.8
  194.3 0.0 copy-start.9
  194.3 0.0 copy-start.2
  194.3 0.0 copy-start.3
  194.3 1.8 bitcast_reduce_fusion
  196.1 0.0 copy-done.8
  196.1 0.0 copy-done.9
  196.1 0.1 pad_add_fusion
  196.2 0.1 broadcast_compare_fusion
  196.3 0.1 select_bitcast_fusion
  196.3 0.8 copy.55
  197.2 0.0 copy-done.2
  197.2 0.0 copy-done.3
  197.2 0.4 fusion.1
  197.6 0.7 copy.56
  198.3 0.0 copy-start.1
  198.3 5.1 %copy.70 = bf16[4,1,1024,576]{2,3,1,0:T(8,128)(2,1)} copy(bf16[4,1,1024,576]{2,3,1,0:T(8,128)(2,1)} %bitcast.60) | data formatting | bytes 9437184
  203.4 0.0 copy-done.1
  203.4 1.0 copy.71
  (14 shorter events, 0.2 us)
Async XLA Ops:
  0.6 4.2 %copy-start = (bf16[4,10,8,128]{3,2,1,0:T(8,128)(2,1)S(1)}, bf16[4,10,8,128]{3,2,1,0:T(8,128)(2,1)}, u32[]{:S(2)}) copy-start(bf16[4,10,8,128]{3,2,1,0:T(8,128)(2,1)} %param.21) | copy-start | bytes 245764
  2.1 4.4 %copy-start.7 = (s32[4]{0:T(128)}, s32[4]{0:T(128)S(1)}, u32[]{:S(2)}) copy-start(s32[4]{0:T(128)S(1)} %get-tuple-element.26.sources) | copy-start | bytes 52
  3.9 2.5 %copy-start.4 = (bf16[4,10,8,64]{3,2,1,0:T(8,128)(2,1)S(1)}, bf16[4,10,8,64]{3,2,1,0:T(8,128)(2,1)}, u32[]{:S(2)}) copy-start(bf16[4,10,8,64]{3,2,1,0:T(8,128)(2,1)} %param.22) | copy-start | bytes 122884
  6.4 1.2 copy-start.5
  7.6 2.4 %copy-start.6 = (bf16[4,10,4]{1,2,0:T(4,128)(2,1)S(1)}, bf16[4,10,4]{1,2,0:T(4,128)(2,1)}, u32[]{:S(2)}) copy-start(bf16[4,10,4]{1,2,0:T(4,128)(2,1)} %param.26) | copy-start | bytes 964
  194.2 1.8 copy-start.8
  194.3 1.8 copy-start.9
  194.3 2.9 %copy-start.2 = (bf16[8,512,128]{2,1,0:T(8,128)(2,1)S(1)}, bf16[8,512,128]{2,1,0:T(8,128)(2,1)}, u32[]{:S(2)}) copy-start(bf16[8,512,128]{2,1,0:T(8,128)(2,1)} %param.24) | copy-start | bytes 3145732
  194.3 2.9 %copy-start.3 = (bf16[10,32,512]{2,1,0:T(8,128)(2,1)S(1)}, bf16[10,32,512]{2,1,0:T(8,128)(2,1)}, u32[]{:S(2)}) copy-start(bf16[10,32,512]{2,1,0:T(8,128)(2,1)} %get-tuple-element.11) | copy-start | bytes 983044
  198.3 5.1 %copy-start.1 = (bf16[4,16,64,128]{3,2,1,0:T(8,128)(2,1)S(1)}, bf16[4,16,64,128]{3,2,1,0:T(8,128)(2,1)}, u32[]{:S(2)}) copy-start(bf16[4,16,64,128]{3,2,1,0:T(8,128)(2,1)} %get-tuple-element.9) | copy-start | bytes 3145732

commit v4 on v3

--- a/solution.py
+++ b/solution.py
@@ -25,9 +25,9 @@
 
 
 def kernel(
-    chosen, sources, limits, lat, idx, qown, wown, reslat, residx, bias,
+    destination, arrive_len, res_len, lat, idx, wown, reslat, residx, w_uk, q_nope, q_rope, idx_query, selected,
     out_lat, out_idx, out_is, out_latent, a_idx, a_lat,
-    ay_bufs, b_idx, b_lat, loads, pack_x, pack_y, unpacked, zs_idx, zs_lat, zrecvs, q_all, w_all, iq_buf, kbuf, ki_res, kfin, kifin, numer, stats,
+    qown, w_buf, live, idx_in, w_idx, ay_bufs, b_idx, b_lat, loads, pack_x, pack_y, unpacked, zs_idx, zs_lat, zrecvs, q_all, w_all, iq_buf, kbuf, ki_res, kfin, kifin, numer, stats,
     ra, rsa, nb_buf, stb, rb, rsb, fbuf,
     sa_s, sa_r, sb_s, sb_r, sz_s, sz_r, own_a, own_b, lat_sem, load_sem, out_sem, kb_sem,
     ag_s, ag_r, aw_s, aw_r, rs_s, rs_r,
@@ -50,6 +50,23 @@
             device_id=target, device_id_type=MESH,
         )
 
+    def chosen(group):
+        k = jnp.int32(0)
+        for n in range(1, NEW):
+            k = jnp.maximum(k, jnp.where(destination[req * NEW + n] == group, n, 0))
+        return k
+
+    def source(k):
+        s = jnp.int32(0)
+        for n in range(1, N_REQ):
+            s = jnp.maximum(s, jnp.where(destination[n * NEW + k] == req, n, 0))
+        return s
+
+    sources = [source(k) for k in range(NEW)]
+    limits = [arrive_len[sources[k] * NEW + k] for k in range(NEW)]
+
+    load_idx = pltpu.make_async_copy(idx, idx_in, load_sem.at[3])
+    load_idx.start()
     barrier = pltpu.get_barrier_semaphore()
     for delta in range(1, N_REQ):
         pl.semaphore_signal(barrier, 1, device_id=((req + delta) % N_REQ, pos), device_id_type=MESH)
@@ -75,8 +92,7 @@
 
     def a_source(i, coord):
         if i < N_IDX:
-            rows = pl.ds(i * HALF, HALF)
-            return idx.at[:, :, coord, rows] if first_axis(i) == 0 else idx.at[:, coord, :, rows]
+            return w_idx.at[i, :, :, coord] if first_axis(i) == 0 else w_idx.at[i, :, coord]
         if first_axis(i) == 0:
             return pack_x.at[(i - N_IDX) // 2 % 2, coord]
         return lat.at[:, depth(i), pl.ds(pl.multiple_of(coord * 256, 256), 256)]
@@ -199,6 +215,23 @@
             copy.start()
         own_copy_b(i).start()
 
+    def stage_z(i, block):
+        def stage(delta, carry):
+            z_send(i)[delta - 1] = block(chosen((req + delta) % N_REQ))
+            copy_z(i, delta).start()
+            return carry
+
+        lax.fori_loop(1, N_REQ, stage, 0)
+        zrecvs[i][req] = block(chosen(req))
+
+    def index_to_z(i):
+        stage_z(i, lambda k: idx_in[k, :, :, i * HALF : (i + 1) * HALF])
+
+    def index_to_a(i):
+        for k in range(NEW):
+            w_idx[i, k] = zrecvs[i][sources[k]]
+        start_a(i)
+
     def b_to_z(i):
         own_copy_b(i).wait()
         for copy in copies_b(i):
@@ -206,31 +239,25 @@
         if i >= N_IDX + RING:
             drain("z", i - RING)
         buf = b_slot(i)
-        if i >= N_IDX:
-            def unpack(row, carry):
-                for pair in range(2):
-                    for kp in range(2):
-                        if first_axis(i) == 0:
-                            even, odd = buf[row, 2 * pair, kp], buf[row, 2 * pair + 1, kp]
-                        else:
-                            even, odd = buf[2 * pair, row, kp], buf[2 * pair + 1, row, kp]
-                        lows, highs = swapped(even, odd)
-                        unpacked[2 * kp, :, lane_tile(row * 2 + pair)] = lows
-                        unpacked[2 * kp + 1, :, lane_tile(row * 2 + pair)] = highs
-                return carry
-
-            lax.fori_loop(0, SIDE, unpack, 0)
+
+        def unpack(row, carry):
+            for pair in range(2):
+                for kp in range(2):
+                    if first_axis(i) == 0:
+                        even, odd = buf[row, 2 * pair, kp], buf[row, 2 * pair + 1, kp]
+                    else:
+                        even, odd = buf[2 * pair, row, kp], buf[2 * pair + 1, row, kp]
+                    lows, highs = swapped(even, odd)
+                    unpacked[2 * kp, :, lane_tile(row * 2 + pair)] = lows
+                    unpacked[2 * kp + 1, :, lane_tile(row * 2 + pair)] = highs
+            return carry
+
+        lax.fori_loop(0, SIDE, unpack, 0)
 
         def block(k):
-            return buf[:, :, k] if i < N_IDX else unpacked[k]
-
-        def stage(delta, carry):
-            z_send(i)[delta - 1] = block(chosen[(req + delta) % N_REQ])
-            copy_z(i, delta).start()
-            return carry
-
-        lax.fori_loop(1, N_REQ, stage, 0)
-        zrecvs[i][req] = block(chosen[req])
+            return unpacked[k]
+
+        stage_z(i, block)
 
     def wait_z(i):
         for delta in range(1, N_REQ):
@@ -242,13 +269,17 @@
         return pltpu.make_async_copy(kfin, out_lat, out_sem.at[1])
 
     def finalize_idx(i):
+        own_copy_b(i).wait()
+        for copy in copies_b(i):
+            copy.wait_recv()
+
         def page(n, carry):
             outer, inner = n // SIDE, n % SIDE
             l = outer * SIDE + inner if first_axis(i) == 0 else inner * SIDE + outer
             base = (l * (SIDE * SIDE) + pos) * PAGE + i * HALF
             row = lax.broadcasted_iota(jnp.int32, (HALF, 128), 0)
             for k in range(NEW):
-                tile = zrecvs[i][sources[k], outer, inner].astype(F32)
+                tile = b_idx[i][outer, inner, k].astype(F32)
                 value = jnp.where(row + base < limits[k], tile, 0.0).astype(BF)
                 kifin[k, l, i * HALF : (i + 1) * HALF, :] = value
             return carry
@@ -256,9 +287,6 @@
         lax.fori_loop(0, SIDE * SIDE, page, 0)
 
     def finalize(i):
-        if i < N_IDX:
-            return finalize_idx(i)
-
         def tiles(n, carry):
             lane = lax.broadcasted_iota(jnp.int32, (DEPTH, 128), 1)
             logical = (2 * n + lane // PAGE) * (SIDE * SIDE * PAGE) + pos * PAGE + lane % PAGE
@@ -322,10 +350,43 @@
 
     own_q = pltpu.make_async_copy(qown, q_all.at[y, x], load_sem.at[0])
     own_w = pltpu.make_async_copy(wown, w_all.at[y, x], load_sem.at[1])
+    load_w = pltpu.make_async_copy(w_uk, w_buf, load_sem.at[4])
     load_ki = pltpu.make_async_copy(residx, ki_res, load_sem.at[2])
 
     def load_k(b):
         return pltpu.make_async_copy(reslat.at[b], kbuf.at[b % 2], kb_sem.at[b])
+
+    def absorb():
+        rows = BATCH * HEADS_DEV
+        head = lax.broadcasted_iota(jnp.int32, (rows, KV), 0) % HEADS_DEV
+        for pair in range(STEPS // 2):
+            blocks = []
+            for t in (2 * pair, 2 * pair + 1):
+                q = q_nope[t].reshape(rows, NOPE)
+                total = jnp.zeros((rows, KV), F32)
+                for h in range(HEADS_DEV):
+                    part = jnp.dot(q, w_buf[h], preferred_element_type=F32)
+                    total = jnp.where(head == h, part, total)
+                keys = idx_query[t].astype(F32)
+                halves = jnp.concatenate([keys[..., :ROPE], keys[..., ROPE:]], axis=1)
+                tail = jnp.concatenate([q_rope[t].astype(F32), halves], axis=2)
+                blocks.append(
+                    jnp.concatenate([total.reshape(BATCH, HEADS_DEV, KV), tail], axis=2)
+                )
+            block = jnp.concatenate(blocks, axis=1).astype(BF)
+            qown[:, pair * 16 : (pair + 1) * 16, :] = block
+
+    def find_live(b):
+        page = lax.broadcasted_iota(jnp.int32, (STEPS, CTX_DEV), 1) // PAGE * (SIDE * SIDE) + pos
+        wanted = selected[b]
+        found = wanted[:, 0:1] == page
+        for n in range(1, wanted.shape[1]):
+            found = found | (wanted[:, n : n + 1] == page)
+        bias = jnp.where(found, 0.0, -1e30)
+        for t in range(STEPS):
+            live[t * HEADS_DEV : (t + 1) * HEADS_DEV, :] = jnp.broadcast_to(
+                bias[t : t + 1], (HEADS_DEV, CTX_DEV)
+            )
 
     def as_row(column):
         size = column.shape[0]
@@ -340,12 +401,13 @@
 
     def attend(b, g, keys):
         b0, half = GROUPS[g][0], STAT_ROWS[g] // 2
+        find_live(b)
 
         def part(n, carry):
             q = q_all[pl.ds(2 * n, 2), :, b, :, 0:LAT].reshape(2 * SIDE * QROWS, LAT)
             k = keys()
             s = jnp.dot(q, k, preferred_element_type=F32)
-            s = (s * SCALE).reshape(2 * SIDE, QROWS, CTX_DEV) + bias[b][None]
+            s = (s * SCALE).reshape(2 * SIDE, QROWS, CTX_DEV) + live[...][None]
             s = s.reshape(2 * SIDE * QROWS, CTX_DEV)
             top = jnp.maximum(jnp.max(s, axis=1, keepdims=True), -1e29)
             e = jnp.exp(s - top)
@@ -361,7 +423,7 @@
 
         lax.fori_loop(0, 2, part, 0)
 
-    def index_scores(b, keys):
+    def index_scores(b, length, keys):
         shape = (SIDE * SIDE // 2, STEPS, HEADS_DEV, 128)
         both = q_all[:, :, b, :, KV:QW].astype(F32).reshape((SIDE * SIDE // 2, 2) + shape[1:])
         even, odd = both[:, 0].reshape(-1, 8, 128), both[:, 1].reshape(-1, 8, 128)
@@ -385,7 +447,13 @@
             )
             value = jnp.maximum(logits, 0.0) * weight
             cols = pl.ds(pl.multiple_of(n * 256, 256), 256)
-            out_is[b, :, cols] = jnp.sum(value.reshape(SIDE * SIDE // 2, QROWS, 256), axis=0)
+            value = jnp.sum(value.reshape(SIDE * SIDE // 2, QROWS, 256), axis=0)
+            value = jnp.sum(value.reshape(STEPS, HEADS_DEV, 256), axis=1) * IDIM ** (-0.5)
+            lane = lax.broadcasted_iota(jnp.int32, (STEPS, 256), 1) + n * 256
+            logical = lane // PAGE * (SIDE * SIDE * PAGE) + pos * PAGE + lane % PAGE
+            value = jnp.where(logical < length, value, 0.0)
+            for t in range(STEPS):
+                out_is[t, b, :, cols] = value[t : t + 1]
             return carry
 
         lax.fori_loop(0, CTX_DEV // 256, part, 0)
@@ -400,10 +468,10 @@
         attend(RES + k, g, lambda: kfin[k])
 
     def index_res(b):
-        index_scores(b, lambda n: ki_res[b, pl.ds(pl.multiple_of(n * 256, 256), 256)])
+        index_scores(b, res_len[b], lambda n: ki_res[b, pl.ds(pl.multiple_of(n * 256, 256), 256)])
 
     def index_new(k):
-        index_scores(RES + k, lambda n: kifin[k, pl.ds(n * 4, 4)].reshape(256, IDIM))
+        index_scores(RES + k, limits[k], lambda n: kifin[k, pl.ds(n * 4, 4)].reshape(256, IDIM))
 
     def lanes(way):
         return pl.ds(way * 256, 256)
@@ -514,32 +582,32 @@
 
     load_lat(N_IDX).start()
     load_lat(N_IDX + 2).start()
-    start_a(0)
-    start_a(1)
-    own_q.start()
+    load_w.start()
     own_w.start()
+    load_idx.wait()
+    index_to_z(0)
+    index_to_z(1)
+    start_a(2)
+    start_a(3)
     load_ki.start()
     load_k(0).start()
     load_k(1).start()
-    start_a(2)
-    start_a(3)
     stats[...] = jnp.zeros_like(stats)
-    a_to_b(0)
-    a_to_b(1)
+    start_a(4)
+    a_to_b(2)
+    a_to_b(3)
+    load_w.wait()
+    absorb()
+    own_q.start()
     start(gather_near(0) + weight_copies(0))
-    start_a(4)
-    b_to_z(0)
-    a_to_b(2)
     start_a(5)
-    b_to_z(1)
-    a_to_b(3)
+    b_to_z(2)
+    a_to_b(4)
     own_q.wait()
     own_w.wait()
     arrived(gather_near(0) + weight_copies(0))
     start(gather_far(0) + weight_copies(1))
     start_a(6)
-    b_to_z(2)
-    a_to_b(4)
 
     for i in range(N_CH):
         wait_z(i)
@@ -549,15 +617,19 @@
             a_to_b(i + 5)
         if i + 7 < N_CH:
             start_a(i + 7)
-        finalize(i)
+        if i < N_IDX:
+            index_to_a(i)
+        else:
+            finalize(i)
         if i == 0:
             arrived(gather_far(0))
             start(gather_near(1))
-        elif i == 1:
-            out_copies("idx").start()
         elif i == 2:
             arrived(gather_near(1))
             start(gather_far(1))
+            a_to_b(0)
+        elif i == 3:
+            a_to_b(1)
         elif i == 4:
             arrived(gather_far(1) + weight_copies(1))
             attend_res(0)
@@ -567,6 +639,9 @@
             attend_res(3)
             load_ki.wait()
             index_res(0)
+            finalize_idx(0)
+            finalize_idx(1)
+            out_copies("idx").start()
         elif i == 6:
             attend_res(4)
             attend_res(5)
@@ -631,14 +706,19 @@
         out_shape=(
             jax.ShapeDtypeStruct((NEW, LAT, CTX_DEV), BF),
             jax.ShapeDtypeStruct((NEW, PG_LOC, PAGE, IDIM), BF),
-            jax.ShapeDtypeStruct((BATCH, QROWS, CTX_DEV), F32),
+            jax.ShapeDtypeStruct((STEPS, BATCH, 1, CTX_DEV), F32),
             jax.ShapeDtypeStruct((BATCH, QROWS, KV), BF),
             jax.ShapeDtypeStruct((N_IDX, SIDE, NEW, SIDE, HALF, 128), BF),
             jax.ShapeDtypeStruct((N_XF, SIDE, 2, SIDE, DEPTH, 128), BF),
         ),
-        in_specs=[smem] * 3 + [hbm] * 6 + [vmem],
+        in_specs=[smem] * 3 + [hbm] * 6 + [vmem] * 4,
         out_specs=(hbm, hbm, vmem, vmem, hbm, hbm),
         scratch_shapes=[
+            pltpu.VMEM((BATCH, QROWS, QW), BF),
+            pltpu.VMEM((HEADS_DEV, NOPE, KV), BF),
+            pltpu.VMEM((QROWS, CTX_DEV), F32),
+            pltpu.VMEM((NEW, SIDE, SIDE, PAGE, IDIM), BF),
+            pltpu.VMEM((N_IDX, NEW) + tile, BF),
             (pltpu.VMEM((SIDE, NEW, DEPTH, 256), BF),) * (N_LAT - N_XF),
             (pltpu.VMEM((SIDE, SIDE, NEW, HALF, 128), BF),) * N_IDX,
             (pltpu.VMEM((SIDE, SIDE, 2, DEPTH, 128), BF),) * N_LAT,
@@ -668,7 +748,7 @@
             pltpu.VMEM((SIDE, 8, SIDE * 128), F32),
             dma((N_CH, 3)), dma((N_CH, 3)), dma((N_CH, 3)), dma((N_CH, 3)),
             dma((N_CH, N_REQ - 1)), dma((N_CH, N_REQ - 1)),
-            dma((N_CH,)), dma((N_CH,)), dma((N_XF,)), dma((3,)), dma((2,)), dma((RES,)),
+            dma((N_CH,)), dma((N_CH,)), dma((N_XF,)), dma((5,)), dma((2,)), dma((RES,)),
             dma((2, 2, 2, 2)), dma((2, 2, 2, 2)), dma((2, 3)), dma((2, 3)),
             dma((n_groups, 2, 2, 2, 3)), dma((n_groups, 2, 2, 2, 3)),
         ],
@@ -683,44 +763,16 @@
     res_latent, res_index, res_len, arrive_latent, arrive_index, arrive_len, destination,
     q_nope, q_rope, w_uk, w_uv, idx_query, idx_weight, selected,
 ):
-    req_index = lax.axis_index("req")
-    pos_index = lax.axis_index("pos")
-    routing = destination.reshape(N_REQ, NEW)
-    group_ids = jnp.arange(N_REQ, dtype=jnp.int32)
-    arrival_ids = jnp.arange(NEW, dtype=jnp.int32)
-    matches = routing[req_index][None, :] == group_ids[:, None]
-    chosen = jnp.sum(jnp.where(matches, arrival_ids[None, :], 0), axis=1)
-    sources = jnp.sum(jnp.where(routing == req_index, group_ids[:, None], 0), axis=0)
-    new_lengths = arrive_len[sources * NEW + arrival_ids]
-
-    absorbed = jnp.einsum("sbhn,hnc->sbhc", q_nope, w_uk, preferred_element_type=F32).astype(BF)
-    halves = jnp.concatenate([idx_query[..., : IDIM // 2], idx_query[..., IDIM // 2 :]], axis=2)
-    queries = jnp.concatenate([absorbed, q_rope, halves], axis=-1)
-    queries = queries.transpose(1, 0, 2, 3).reshape(BATCH, QROWS, QW)
     weights = jnp.concatenate([idx_weight, idx_weight], axis=2).astype(F32)
     weights = weights.transpose(1, 0, 2).reshape(BATCH, QROWS)
     weights = jnp.pad(weights, ((0, 16 - BATCH), (0, 128 - QROWS)))
 
-    here = (selected % (SIDE * SIDE) == pos_index)[..., None]
-    slots = jnp.arange(PG_LOC, dtype=jnp.int32)
-    live = jnp.any(here & (selected[..., None] // (SIDE * SIDE) == slots), axis=2)
-    bias = jnp.where(jnp.repeat(live, PAGE, axis=-1), 0.0, -1e30).astype(F32)
-    bias = jnp.broadcast_to(
-        bias.transpose(1, 0, 2)[:, :, None, :], (BATCH, STEPS, HEADS_DEV, CTX_DEV)
-    ).reshape(BATCH, QROWS, CTX_DEV)
-
-    new_latent, new_index, raw, latent, _, _ = run_kernel(
-        chosen.astype(jnp.int32), sources.astype(jnp.int32), new_lengths,
+    new_latent, new_index, index_scores, latent, _, _ = run_kernel(
+        destination, arrive_len, res_len,
         arrive_latent.transpose(0, 2, 1), arrive_index.reshape(NEW, SIDE, SIDE, PAGE, IDIM),
-        queries, weights, res_latent[:, 0].transpose(0, 2, 1), res_index[:, 0], bias,
+        weights, res_latent[:, 0].transpose(0, 2, 1), res_index[:, 0], w_uk,
+        q_nope, q_rope, idx_query, selected.transpose(1, 0, 2),
     )
-
-    scored = jnp.sum(raw.reshape(BATCH, STEPS, HEADS_DEV, CTX_DEV), axis=2) * IDIM ** (-0.5)
-    lengths = jnp.concatenate([res_len, new_lengths])
-    offsets = jnp.arange(CTX_DEV, dtype=jnp.int32)
-    logical = (offsets // PAGE * (SIDE * SIDE) + pos_index) * PAGE + offsets % PAGE
-    index_scores = jnp.where(logical[None, None, :] < lengths[:, None, None], scored, 0.0)
-    index_scores = index_scores.transpose(1, 0, 2)[:, :, None, :]
 
     latent = latent.reshape(BATCH, STEPS, HEADS_DEV, KV)
     head_out = jnp.einsum("bshc,hcd->sbhd", latent, w_uv, preferred_element_type=F32).astype(BF)

time: 206 us -> 185 us (0.90)
  Pallas kernels: 183 us -> 173 us
  local copies, waits for them, and re-layouts: 13.9 us -> 7.54 us
  other arithmetic: 4.27 us -> 1.4 us
    pallas_call x1, Pallas kernels: 183 us -> 173 us  [run_kernel(): pl.pallas_call(kernel, out_shape=(jax.ShapeDtypeStruct((NEW, LAT, CTX_DEV...]
    reduce_sum x2 -> x0, other arithmetic: 2.41 us -> none  [the longest x1 1.78 us: body(): jnp.sum(raw.reshape(BATCH, STEPS, HEADS_DEV, CTX_DEV), axis=2)]
    unnamed x27 -> x8, local copies, waits for them, and re-layouts: 7.72 us -> 7.46 us
where the time goes in v4:
time: 185 us
  Pallas kernels  173 us (94%)
  local copies, waits for them, and re-layouts  7.54 us (4%)
    pallas_call x1, Pallas kernels, run_kernel(): pl.pallas_call(kernel, out_shape=(jax.ShapeDtypeStruct((NEW, LAT, CTX_DEV...  173 us
    unnamed x8, local copies, waits for them, and re-layouts  7.46 us

profile of v4, /device:TPU:0, one launch (start us, length us, event | category | flops | bytes accessed | tf_op | source)
XLA Modules:
  0.0 184.6 jit_solution(13547729362361787980)
XLA Ops:
  0.6 0.8 maximum_bitcast_fusion
  1.4 0.1 copy.29
  1.5 0.6 pad_convert_fusion.wown
  2.1 173.3 %decode_step.1 = (bf16[4,576,1024]{2,1,0:T(8,128)(2,1)}, bf16[4,16,64,128]{3,2,1,0:T(8,128)(2,1)}, f32[4,10,1,1024]{3,2,1,0:T(1,128)}, bf16[10,32,512]{2,1,0:T(8...) custom-call(s32[32]{0:T(128)} %destination.1, s32[32]{0:T(128)} %arrive_len.1, ...), custom_call_target="tpu_custom_call" | custom-call | tf_op jit(solution)/shard_map/decode_step/pallas_call | solution.py:704
  175.4 1.7 fusion
  177.1 0.7 copy.27
  177.8 0.0 copy-start
  177.8 0.0 copy-start.1
  177.8 5.1 %copy.35 = bf16[4,1,1024,576]{2,3,1,0:T(8,128)(2,1)} copy(bf16[4,1,1024,576]{2,3,1,0:T(8,128)(2,1)} %bitcast.28) | data formatting | bytes 9437184
  183.0 0.0 copy-done
  183.0 1.0 copy.36
  183.9 0.0 copy-done.1
  183.9 0.7 copy.37
Async XLA Ops:
  177.8 5.1 %copy-start = (bf16[4,16,64,128]{3,2,1,0:T(8,128)(2,1)S(1)}, bf16[4,16,64,128]{3,2,1,0:T(8,128)(2,1)}, u32[]{:S(2)}) copy-start(bf16[4,16,64,128]{3,2,1,0:T(8,128)(2,1)} %get-tuple-element.9) | copy-start | bytes 3145732
  177.8 6.1 %copy-start.1 = (f32[4,10,1,1024]{3,2,1,0:T(1,128)S(1)}, f32[4,10,1,1024]{3,2,1,0:T(1,128)}, u32[]{:S(2)}) copy-start(f32[4,10,1,1024]{3,2,1,0:T(1,128)} %get-tuple-element.26) | copy-start | bytes 491524

commit v5 on v4

--- a/solution.py
+++ b/solution.py
@@ -19,9 +19,9 @@
 N_IDX, N_LAT, DEPTH = 2, LAT // 64, 64
 N_CH = N_IDX + N_LAT
 N_XF = (N_LAT + 1) // 2
-RING = 3
-GROUPS = ((0, 6), (6, 1), (7, 1), (8, 1), (9, 1))
-STAT_ROWS = (16, 8, 8, 8, 8)
+RING = 4
+GROUPS = ((0, 3), (6, 1), (7, 1), (8, 1), (9, 1), (3, 3))
+STAT_ROWS = (8, 8, 8, 8, 8, 8)
 
 
 def kernel(
@@ -460,7 +460,7 @@
 
     def attend_res(b):
         load_k(b).wait()
-        attend(b, 0, lambda: kbuf[b % 2])
+        attend(b, 0 if b < 3 else 5, lambda: kbuf[b % 2])
         if b + 2 < RES:
             load_k(b + 2).start()
 
@@ -608,15 +608,19 @@
     arrived(gather_near(0) + weight_copies(0))
     start(gather_far(0) + weight_copies(1))
     start_a(6)
+    a_to_b(5)
+    start_a(7)
+    b_to_z(3)
+    b_to_z(4)
 
     for i in range(N_CH):
         wait_z(i)
-        if i + 3 < N_CH:
-            b_to_z(i + 3)
-        if i + 5 < N_CH:
-            a_to_b(i + 5)
-        if i + 7 < N_CH:
-            start_a(i + 7)
+        if 0 < i < N_CH - 4:
+            b_to_z(i + 4)
+        if i + 6 < N_CH:
+            a_to_b(i + 6)
+        if i + 8 < N_CH:
+            start_a(i + 8)
         if i < N_IDX:
             index_to_a(i)
         else:
@@ -636,44 +640,47 @@
             attend_res(1)
         elif i == 5:
             attend_res(2)
+            for way in range(2):
+                start_reduce(0, 0, way)
             attend_res(3)
-            load_ki.wait()
-            index_res(0)
-            finalize_idx(0)
-            finalize_idx(1)
-            out_copies("idx").start()
         elif i == 6:
             attend_res(4)
             attend_res(5)
             for way in range(2):
-                start_reduce(0, 0, way)
+                start_reduce(5, 0, way)
+            load_ki.wait()
+            index_res(0)
+        elif i == 7:
+            for way in range(2):
+                combine_a(0, way)
             index_res(1)
-        elif i == 7:
-            for b in range(2, RES):
-                index_res(b)
+            index_res(2)
+            finalize_idx(0)
+            finalize_idx(1)
+            out_copies("idx").start()
         elif i == 8:
             for way in range(2):
-                combine_a(0, way)
+                combine_a(5, way)
+            index_res(3)
+            index_res(4)
+        elif i == 9:
+            index_res(5)
             index_new(0)
-            index_new(1)
-        elif i == 9:
-            index_new(2)
-            index_new(3)
-        if i == N_CH - 1:
-            out_copies("lat").start()
-            attend_new(0, 1)
-            for way in range(2):
-                start_reduce(1, 0, way)
-            attend_new(1, 2)
-            for way in range(2):
-                start_reduce(2, 0, way)
             for way in range(2):
                 combine_b(0, way)
-    for k in (2, 3):
+            index_new(1)
+            for way in range(2):
+                combine_b(5, way)
+    out_copies("lat").start()
+    for k in range(NEW):
         attend_new(k, k + 1)
         for way in range(2):
             start_reduce(k + 1, 0, way)
-    for g in (1, 2, 3, 4):
+    index_new(2)
+    for way in range(2):
+        combine_a(1, way)
+    index_new(3)
+    for g in (2, 3, 4):
         for way in range(2):
             combine_a(g, way)
     for g in (1, 2, 3, 4):

time: 185 us -> 179 us (0.968)
  Pallas kernels: 173 us -> 167 us
    pallas_call x1, Pallas kernels: 173 us -> 167 us  [run_kernel(): pl.pallas_call(kernel, out_shape=(jax.ShapeDtypeStruct((NEW, LAT, CTX_DEV...]
where the time goes in v5:
time: 179 us
  Pallas kernels  167 us (93%)
  local copies, waits for them, and re-layouts  7.54 us (4%)
    pallas_call x1, Pallas kernels, run_kernel(): pl.pallas_call(kernel, out_shape=(jax.ShapeDtypeStruct((NEW, LAT, CTX_DEV...  167 us
    unnamed x8, local copies, waits for them, and re-layouts  7.46 us

profile of v5, /device:TPU:0, one launch (start us, length us, event | category | flops | bytes accessed | tf_op | source)
XLA Modules:
  0.0 178.6 jit_solution(15632536128987651041)
XLA Ops:
  0.6 0.8 maximum_bitcast_fusion
  1.4 0.1 copy.29
  1.5 0.6 pad_convert_fusion.wown
  2.1 167.3 %decode_step.1 = (bf16[4,576,1024]{2,1,0:T(8,128)(2,1)}, bf16[4,16,64,128]{3,2,1,0:T(8,128)(2,1)}, f32[4,10,1,1024]{3,2,1,0:T(1,128)}, bf16[10,32,512]{2,1,0:T(8...) custom-call(s32[32]{0:T(128)} %destination.1, s32[32]{0:T(128)} %arrive_len.1, ...), custom_call_target="tpu_custom_call" | custom-call | tf_op jit(solution)/shard_map/decode_step/pallas_call | solution.py:711
  169.4 1.7 fusion
  171.1 0.7 copy.27
  171.8 0.0 copy-start
  171.8 0.0 copy-start.1
  171.8 5.1 %copy.35 = bf16[4,1,1024,576]{2,3,1,0:T(8,128)(2,1)} copy(bf16[4,1,1024,576]{2,3,1,0:T(8,128)(2,1)} %bitcast.28) | data formatting | bytes 9437184
  177.0 0.0 copy-done
  177.0 1.0 copy.36
  177.9 0.0 copy-done.1
  177.9 0.7 copy.37
Async XLA Ops:
  171.8 5.1 %copy-start = (bf16[4,16,64,128]{3,2,1,0:T(8,128)(2,1)S(1)}, bf16[4,16,64,128]{3,2,1,0:T(8,128)(2,1)}, u32[]{:S(2)}) copy-start(bf16[4,16,64,128]{3,2,1,0:T(8,128)(2,1)} %get-tuple-element.9) | copy-start | bytes 3145732
  171.8 6.1 %copy-start.1 = (f32[4,10,1,1024]{3,2,1,0:T(1,128)S(1)}, f32[4,10,1,1024]{3,2,1,0:T(1,128)}, u32[]{:S(2)}) copy-start(f32[4,10,1,1024]{3,2,1,0:T(1,128)} %get-tuple-element.26) | copy-start | bytes 491524

commit v6 on v5

--- a/solution.py
+++ b/solution.py
@@ -615,12 +615,12 @@
 
     for i in range(N_CH):
         wait_z(i)
-        if 0 < i < N_CH - 4:
-            b_to_z(i + 4)
         if i + 6 < N_CH:
             a_to_b(i + 6)
         if i + 8 < N_CH:
             start_a(i + 8)
+        if 0 < i < N_CH - 4:
+            b_to_z(i + 4)
         if i < N_IDX:
             index_to_a(i)
         else:

time: 179 us -> 179 us (level)
  no operation moved by 1% of the time
where the time goes in v6:
time: 179 us
  Pallas kernels  167 us (93%)
  local copies, waits for them, and re-layouts  7.54 us (4%)
    pallas_call x1, Pallas kernels, run_kernel(): pl.pallas_call(kernel, out_shape=(jax.ShapeDtypeStruct((NEW, LAT, CTX_DEV...  167 us
    unnamed x8, local copies, waits for them, and re-layouts  7.46 us

profile of v6, /device:TPU:0, one launch (start us, length us, event | category | flops | bytes accessed | tf_op | source)
XLA Modules:
  0.0 178.6 jit_solution(12123274731118668957)
XLA Ops:
  0.6 0.8 maximum_bitcast_fusion
  1.4 0.1 copy.29
  1.5 0.6 pad_convert_fusion.wown
  2.1 167.3 %decode_step.1 = (bf16[4,576,1024]{2,1,0:T(8,128)(2,1)}, bf16[4,16,64,128]{3,2,1,0:T(8,128)(2,1)}, f32[4,10,1,1024]{3,2,1,0:T(1,128)}, bf16[10,32,512]{2,1,0:T(8...) custom-call(s32[32]{0:T(128)} %destination.1, s32[32]{0:T(128)} %arrive_len.1, ...), custom_call_target="tpu_custom_call" | custom-call | tf_op jit(solution)/shard_map/decode_step/pallas_call | solution.py:711
  169.4 1.7 fusion
  171.1 0.7 copy.27
  171.8 0.0 copy-start
  171.8 0.0 copy-start.1
  171.8 5.1 %copy.35 = bf16[4,1,1024,576]{2,3,1,0:T(8,128)(2,1)} copy(bf16[4,1,1024,576]{2,3,1,0:T(8,128)(2,1)} %bitcast.28) | data formatting | bytes 9437184
  177.0 0.0 copy-done
  177.0 1.0 copy.36
  177.9 0.0 copy-done.1
  177.9 0.7 copy.37
Async XLA Ops:
  171.8 5.1 %copy-start = (bf16[4,16,64,128]{3,2,1,0:T(8,128)(2,1)S(1)}, bf16[4,16,64,128]{3,2,1,0:T(8,128)(2,1)}, u32[]{:S(2)}) copy-start(bf16[4,16,64,128]{3,2,1,0:T(8,128)(2,1)} %get-tuple-element.9) | copy-start | bytes 3145732
  171.8 6.1 %copy-start.1 = (f32[4,10,1,1024]{3,2,1,0:T(1,128)S(1)}, f32[4,10,1,1024]{3,2,1,0:T(1,128)}, u32[]{:S(2)}) copy-start(f32[4,10,1,1024]{3,2,1,0:T(1,128)} %get-tuple-element.26) | copy-start | bytes 491524
